TPU v7x, 256 devices: a whole 4x4x8 slice. The times are simulated.
256 devices in a mesh: dp: 4 (over x), ctx: 32 (over y, z), head: 2 (over core).
Axes of the slice: x: 4, y: 4, z: 8, core: 2. Of those that a mesh axis runs over, the one named last changes fastest.
Arguments:
- queries: bfloat16 [16384, 32, 128], P(('dp', 'ctx'), 'head'), parts along dimension 0, may hold values from -15 to 15
- key_rows: bfloat16 [16384, 4, 128], P(('dp', 'ctx'), 'head'), parts along dimension 0, may hold values from -15 to 15
- values: bfloat16 [16384, 4, 128], P(('dp', 'ctx'), 'head'), parts along dimension 0, may hold values from -12 to 12
- out_grad: bfloat16 [16384, 32, 128], P(('dp', 'ctx'), 'head'), parts along dimension 0, may hold values from -6 to 6
- doc_lengths: int32 [64], P('dp'), parts along dimension 0, may hold values from 1 to 3072, 4096 in all
Outputs:
- attended: bfloat16 [16384, 32, 128], P(('dp', 'ctx'), 'head'), parts along dimension 0
- query_grad: bfloat16 [16384, 32, 128], P(('dp', 'ctx'), 'head'), parts along dimension 0
- key_grad: bfloat16 [16384, 4, 128], P(('dp', 'ctx'), 'head'), parts along dimension 0
- value_grad: bfloat16 [16384, 4, 128], P(('dp', 'ctx'), 'head'), parts along dimension 0
There are 4 independent parts, one for each index of `dp`. A program takes and returns all parts, laid end to end along the dimension named above; each array names one. Nothing has to cross between parts.
Inputs may be any that keep to these rules, and one draw needn't show every extreme that they name: `doc_lengths`: the lengths sum to 4096; the longest is exactly 3072.
All inputs are finite; a program needn't handle non-finite values.
Results may differ from a plain program's by a relative error of at most 0.03.
Values may be sent and summed in bfloat16 or wider, within the bound.
No kernel may reach another device: no remote copies, remote signals or barrier semaphores. Data moves between devices by JAX's collectives and lax.ppermute only.
A program may use at most 128 MiB of HBM per device.

v0:
```python
import math

import jax
import jax.numpy as jnp
from jax import lax
from jax.sharding import PartitionSpec as P

MASKED_SCORE = -1e30


def doc_index(positions, bounds):
    return jnp.sum((positions[:, None] >= bounds[None, :]).astype(jnp.int32), axis=1)


def doc_opening(positions, bounds, doc_lengths):
    labels = doc_index(positions, bounds)
    openings = bounds - doc_lengths
    ranks = jnp.arange(doc_lengths.shape[0], dtype=jnp.int32)
    return jnp.sum(jnp.where(labels[:, None] == ranks[None, :], openings[None, :], 0), axis=1)


def pair_allowed(query_pos, query_doc, key_pos, key_doc):
    return ((key_pos[None, :] <= query_pos[:, None]) & (key_doc[None, :] == query_doc[:, None]))[
        None, None
    ]


def online_update(running, query_half, key_piece, value_piece, allowed, score_scale):
    row_max, row_total, weighted = running
    scores = (
        jnp.einsum("qagd,kad->agqk", query_half, key_piece, preferred_element_type=jnp.float32)
        * score_scale
    )
    scores = jnp.where(allowed, scores, MASKED_SCORE)
    new_max = jnp.maximum(row_max, jnp.max(scores, axis=-1))
    weights = jnp.where(allowed, jnp.exp(scores - new_max[..., None]), 0.0)
    new_total = jnp.sum(weights, axis=-1)
    added_term = jnp.einsum(
        "agqk,kad->agqd",
        weights.astype(jnp.bfloat16),
        value_piece,
        preferred_element_type=jnp.float32,
    )
    return (new_max, new_total, added_term)


def grad_block(
    query_half, grad_half, log_total, out_dot, key_block, value_block, allowed, score_scale
):
    scores = (
        jnp.einsum("qagd,kad->agqk", query_half, key_block, preferred_element_type=jnp.float32)
        * score_scale
    )
    probs = jnp.where(allowed, jnp.exp(scores - log_total[..., None]), 0.0)
    dprobs = jnp.einsum(
        "qagd,kad->agqk", grad_half, value_block, preferred_element_type=jnp.float32
    )
    dscores = (probs * (dprobs - out_dot[..., None])).astype(jnp.bfloat16)
    query_part = jnp.einsum(
        "agqk,kad->agqd", dscores, key_block, preferred_element_type=jnp.float32
    )
    key_part = (
        jnp.einsum("agqk,qagd->kad", dscores, query_half, preferred_element_type=jnp.float32)
        * score_scale
    )
    value_part = jnp.einsum(
        "agqk,qagd->kad", probs.astype(jnp.bfloat16), grad_half, preferred_element_type=jnp.float32
    )
    return (query_part, key_part, value_part)


def on_device(queries, key_rows, values, out_grad, doc_lengths):
    row_count, query_heads, head_size = queries.shape
    key_heads = key_rows.shape[1]
    group_size = query_heads // key_heads
    half_rows = row_count // 2
    ctx_size = lax.axis_size("ctx")
    key_total = ctx_size * row_count
    ctx_index = lax.axis_index("ctx")
    score_scale = 1.0 / math.sqrt(head_size)
    bounds = jnp.cumsum(doc_lengths)
    local_rows = jnp.arange(row_count, dtype=jnp.int32)
    all_pos = ctx_index * row_count + local_rows
    query_parts, grad_parts, query_pos, query_doc, query_last, query_open = ([], [], [], [], [], [])
    for part_number in range(2):
        rows_here = slice(part_number * half_rows, (part_number + 1) * half_rows)
        positions = all_pos[rows_here]
        query_parts.append(queries[rows_here].reshape(half_rows, key_heads, group_size, head_size))
        grad_parts.append(out_grad[rows_here].reshape(half_rows, key_heads, group_size, head_size))
        query_pos.append(positions)
        query_doc.append(doc_index(positions, bounds))
        query_last.append(jnp.max(positions))
        query_open.append(doc_opening(jnp.min(positions)[None], bounds, doc_lengths)[0])

    def is_live(part_number, key_start):
        live = key_start <= query_last[part_number]
        return live

    def fold_part(running, part_number, key_piece, value_piece, key_pos, key_doc, key_start):
        allowed = pair_allowed(query_pos[part_number], query_doc[part_number], key_pos, key_doc)
        return lax.cond(
            is_live(part_number, key_start),
            lambda: online_update(
                running, query_parts[part_number], key_piece, value_piece, allowed, score_scale
            ),
            lambda: running,
        )

    empty_stats = (
        jnp.full((key_heads, group_size, half_rows), MASKED_SCORE, jnp.float32),
        jnp.zeros((key_heads, group_size, half_rows), jnp.float32),
        jnp.zeros((key_heads, group_size, half_rows, head_size), jnp.float32),
    )
    empty_store = ()
    state_now = (empty_stats, empty_stats, empty_store)
    key_start = jnp.int32(0)
    key_piece = lax.all_gather(key_rows, "ctx", axis=0, tiled=True)
    value_piece = lax.all_gather(values, "ctx", axis=0, tiled=True)
    key_count = key_piece.shape[0]
    key_pos = jnp.arange(key_count, dtype=jnp.int32)
    key_doc = doc_index(key_pos, bounds)
    first_part = fold_part(state_now[0], 0, key_piece, value_piece, key_pos, key_doc, key_start)
    second_part = fold_part(state_now[1], 1, key_piece, value_piece, key_pos, key_doc, key_start)
    stored = state_now[2]
    folded = (first_part, second_part, stored)
    out_parts, log_totals, out_dots = ([], [], [])
    for part_number in range(2):
        row_max, row_total, weighted = folded[part_number]
        attended_part = (weighted / row_total[..., None]).astype(jnp.bfloat16)
        log_totals.append(row_max + jnp.log(row_total))
        grad_turned = jnp.transpose(grad_parts[part_number], (1, 2, 0, 3)).astype(jnp.float32)
        out_dots.append(jnp.sum(grad_turned * attended_part.astype(jnp.float32), axis=-1))
        out_parts.append(
            jnp.transpose(attended_part, (2, 0, 1, 3)).reshape(half_rows, query_heads, head_size)
        )
    whole_keys, whole_values = (
        lax.all_gather(key_rows, "ctx", axis=0, tiled=True),
        lax.all_gather(values, "ctx", axis=0, tiled=True),
    )
    key_block_rows = math.gcd(512, key_total)

    def backward_step(block_number, state_now):
        grads_query = [state_now[0], state_now[1]]
        key_term, value_term = (state_now[2], state_now[3])
        key_start = (block_number * key_block_rows).astype(jnp.int32)
        key_block = lax.dynamic_slice_in_dim(whole_keys, key_start, key_block_rows, 0)
        value_block = lax.dynamic_slice_in_dim(whole_values, key_start, key_block_rows, 0)
        key_pos = key_start + jnp.arange(key_block_rows, dtype=jnp.int32)
        key_doc = doc_index(key_pos, bounds)
        key_sum = jnp.zeros((key_block_rows, key_heads, head_size), jnp.float32)
        value_sum = jnp.zeros((key_block_rows, key_heads, head_size), jnp.float32)
        for part_number in range(2):
            allowed = pair_allowed(query_pos[part_number], query_doc[part_number], key_pos, key_doc)
            query_part, key_part, value_part = lax.cond(
                is_live(part_number, key_start),
                lambda: grad_block(
                    query_parts[part_number],
                    grad_parts[part_number],
                    log_totals[part_number],
                    out_dots[part_number],
                    key_block,
                    value_block,
                    allowed,
                    score_scale,
                ),
                lambda: (
                    jnp.zeros((key_heads, group_size, half_rows, head_size), jnp.float32),
                    jnp.zeros((key_block_rows, key_heads, head_size), jnp.float32),
                    jnp.zeros((key_block_rows, key_heads, head_size), jnp.float32),
                ),
            )
            grads_query[part_number] = grads_query[part_number] + query_part
            key_sum = key_sum + key_part
            value_sum = value_sum + value_part
        key_term = lax.dynamic_update_slice_in_dim(key_term, key_sum, key_start, 0)
        value_term = lax.dynamic_update_slice_in_dim(value_term, value_sum, key_start, 0)
        return (grads_query[0], grads_query[1], key_term, value_term)

    start_state = (
        jnp.zeros((key_heads, group_size, half_rows, head_size), jnp.float32),
        jnp.zeros((key_heads, group_size, half_rows, head_size), jnp.float32),
        jnp.zeros((key_total, key_heads, head_size), jnp.float32),
        jnp.zeros((key_total, key_heads, head_size), jnp.float32),
    )
    finished = lax.fori_loop(0, key_total // key_block_rows, backward_step, start_state)
    key_sums = (
        lax.psum_scatter(
            finished[2].astype(jnp.bfloat16), "ctx", scatter_dimension=0, tiled=True
        ).astype(jnp.float32),
        lax.psum_scatter(
            finished[3].astype(jnp.bfloat16), "ctx", scatter_dimension=0, tiled=True
        ).astype(jnp.float32),
    )
    key_grad = key_sums[0].astype(jnp.bfloat16)
    value_grad = key_sums[1].astype(jnp.bfloat16)
    query_rows = []
    for part_number in range(2):
        scaled = finished[part_number] * score_scale
        query_rows.append(
            jnp.transpose(scaled, (2, 0, 1, 3))
            .reshape(half_rows, query_heads, head_size)
            .astype(jnp.bfloat16)
        )
    attended = jnp.concatenate(out_parts, axis=0)
    query_grad = jnp.concatenate(query_rows, axis=0)
    return (attended, query_grad, key_grad, value_grad)


def solution(mesh):
    placed = (
        P(("dp", "ctx"), "head", None),
        P(("dp", "ctx"), "head", None),
        P(("dp", "ctx"), "head", None),
        P(("dp", "ctx"), "head", None),
        P("dp"),
    )
    return jax.shard_map(
        on_device,
        mesh=mesh,
        in_specs=placed,
        out_specs=(
            P(("dp", "ctx"), "head", None),
            P(("dp", "ctx"), "head", None),
            P(("dp", "ctx"), "head", None),
            P(("dp", "ctx"), "head", None),
        ),
        check_vma=False,
    )
```

profile of v0, /device:TPU:6, one launch (start us, length us, event | category | flops | bytes accessed | tf_op | source)
XLA Modules:
  0.0 534.9 jit_solution(2148743328422113754)
XLA Ops:
  18.2 74.0 %all-gather.3.cloned.1.call-done = bf16[4096,2,128]{2,0,1:T(8,128)(2,1)} async-done(((bf16[128,2,128]{2,0,1:T(8,128)(2,1)}), bf16[4096,2,128]{2,0,1:T(8,128)(2,1)}) %all-gather.3.cloned.1.call-update) | async-done | bytes 2097168 | tf_op jit(solution)/shard_map/all_gather | solution.py:117
  92.2 78.4 %all-gather.5.cloned.1.call-done = bf16[4096,2,128]{2,0,1:T(8,128)(2,1)} async-done(((bf16[128,2,128]{2,0,1:T(8,128)(2,1)}), bf16[4096,2,128]{2,0,1:T(8,128)(2,1)}) %all-gather.5.cloned.1.call-update) | async-done | bytes 2097168 | tf_op jit(solution)/shard_map/all_gather | solution.py:118
  171.5 21.1 %conditional.4 = (f32[2,8,64]{2,1,0:T(8,128)}, f32[2,8,64]{2,1,0:T(8,128)}, f32[2,8,64,128]{3,2,1,0:T(8,128)S(1)}, f32[2,8,64]{2,1,0:T(8,128)S(1)}) conditional(s32[]{:T(128)} %convert_element_type.106, () %tuple.58, (s32[64]{0:T(128)S(1)}, s32[1,1,64,4096]{3,2,1,0:T(8,128)S(1)}, s32[64]{0:T(128)S(1)}, s32[1,1,64,4096]{3,2,1,0:T(8,128)S(1)}, ...), branch_computations={%region_4.5_spmd, %region_5.0_spmd} | conditional | flops 2202795008 | bytes 133988952 | solution.py:101
  171.8 4.4 fusion
  176.8 6.9 %fusion.2 = f32[2,8,64]{2,1,0:T(8,128)} fusion(f32[2,4096,64,8]{1,2,3,0:T(8,128)S(1)} %get-tuple-element.632, f32[2,8,64]{2,1,0:T(8,128)} %broadcast_maximum_fusion, pred[64,4096]{1,0:T(8,128)(4,1)S(1)} %and_bitcast_fusion), kind=kLoop, calls=%fused_computation.4 | loop fusion | flops 20970496 | bytes 17047552 | tf_op jit(solution)/shard_map/cond/branch_1_fun/reduce_sum | solution.py:37
  183.7 8.1 %fusion.3 = f32[2,8,64,128]{3,2,1,0:T(8,128)S(1)} fusion(f32[2,4096,64,8]{1,2,3,0:T(8,128)} %copy-done, f32[2,8,64]{2,1,0:T(8,128)} %broadcast_maximum_fusion, pred[64,4096]{1,0:T(8,128)(4,1)S(1)} %and_bitcast_fusion, bf16[4096,2,128]{2,0,1:T(8,128)(2,1)S(1)} %copy-done.11), kind=kOutput, calls=%fused_computation.5 | convolution fusion | flops 1094713344 | bytes 19664896 | tf_op jit(solution)/shard_map/cond/branch_1_fun/agqk,kad->agqd/dot_general | solution.py:38
  194.0 21.4 %conditional.5 = (f32[2,8,64]{2,1,0:T(8,128)}, f32[2,8,64]{2,1,0:T(8,128)}, f32[2,8,64,128]{3,2,1,0:T(8,128)S(1)}, f32[2,8,64]{2,1,0:T(8,128)S(1)}) conditional(s32[]{:T(128)} %convert_element_type.110, () %tuple.60, (s32[64]{0:T(128)S(1)}, s32[1,1,64,4096]{3,2,1,0:T(8,128)S(1)}, s32[64]{0:T(128)S(1)}, s32[1,1,64,4096]{3,2,1,0:T(8,128)S(1)}, ...), branch_computations={%region_10.11_spmd, %region_11.14_spmd} | conditional | flops 2202795008 | bytes 133988952 | solution.py:101
  194.4 4.4 fusion.12
  199.5 6.9 %fusion.14 = f32[2,8,64]{2,1,0:T(8,128)} fusion(f32[2,4096,64,8]{1,2,3,0:T(8,128)S(1)} %get-tuple-element.634, f32[2,8,64]{2,1,0:T(8,128)} %broadcast_maximum_fusion.1, pred[64,4096]{1,0:T(8,128)(4,1)S(1)} %and_bitcast_fusion.1), kind=kLoop, calls=%fused_computation.19 | loop fusion | flops 20970496 | bytes 17047552 | tf_op jit(solution)/shard_map/cond/branch_1_fun/reduce_sum | solution.py:37
  206.4 8.2 %fusion.15 = f32[2,8,64,128]{3,2,1,0:T(8,128)S(1)} fusion(f32[2,4096,64,8]{1,2,3,0:T(8,128)} %copy-done.1, f32[2,8,64]{2,1,0:T(8,128)} %broadcast_maximum_fusion.1, pred[64,4096]{1,0:T(8,128)(4,1)S(1)} %and_bitcast_fusion.1, bf16[4096,2,128]{2,0,1:T(8,128)(2,1)S(1)} %copy-done.12), kind=kOutput, calls=%fused_computation.20 | convolution fusion | flops 1094713344 | bytes 19664896 | tf_op jit(solution)/shard_map/cond/branch_1_fun/agqk,kad->agqd/dot_general | solution.py:38
  216.6 1.6 fusion.46
  219.9 2.4 broadcast.171.clone
  222.3 2.5 broadcast.171.clone2
  224.8 74.8 %while.20 = (s32[]{:T(128)}, f32[2,8,64,128]{3,2,1,0:T(8,128)}, f32[2,8,64,128]{3,2,1,0:T(8,128)}, bf16[4096,2,128]{2,1,0:T(2,128)(2,1)}, bf16[4096,2,128]{2,1,0...) while((s32[]{:T(128)}, f32[2,8,64,128]{3,2,1,0:T(8,128)}, ...), condition=%wide.region_22.23_spmd.clone, body=%wide.region_16.22_spmd.clone.sunk | while | flops 1350787072 | bytes 38703024 | solution.py:185
  228.2 5.2 conditional.10
  234.1 4.4 conditional.11
  245.7 2.4 select_add_fusion.3
  254.0 2.4 select_add_fusion.3
  262.3 2.4 select_add_fusion.3
  270.7 2.4 select_add_fusion.3
  279.0 2.4 select_add_fusion.3
  287.4 2.4 select_add_fusion.3
  295.7 2.4 select_add_fusion.3
  304.1 222.7 %all-reduce.5.cloned.1.call-done = (bf16[4096,2,128]{2,1,0:T(2,128)(2,1)}, bf16[4096,2,128]{2,1,0:T(2,128)(2,1)}) async-done(((bf16[4096,2,128]{2,1,0:T(2,128)(2,1)}, bf16[4096,2,128]{2,1,0:T(2,128)(2,1)}), (bf16[4096,2,128]{2,1,0:T(2,128)(2,1)}, bf16[4096,2,128]{2,1,0:T(2,128)(2,1)})) %all-reduce.5.cloned.1.call-update) | async-done | bytes 4194320
  (370 shorter events, 71.7 us)
Async XLA Ops:
  7.2 7.2 %copy-start.13 = (bf16[128,16,128]{2,1,0:T(8,128)(2,1)S(1)}, bf16[128,16,128]{2,1,0:T(8,128)(2,1)}, u32[]{:S(2)}) copy-start(bf16[128,16,128]{2,1,0:T(8,128)(2,1)} %param.15) | copy-start | bytes 1572868
  7.2 85.0 %all-gather.3.cloned.1.call-start = ((), (), s32[]{:S(2)}) async-start(), calls=%async_computation | async-start | bytes 2162688 | tf_op jit(solution)/shard_map/all_gather | solution.py:117
  8.8 161.8 %all-gather.5.cloned.1.call-start = ((), (), s32[]{:S(2)}) async-start(), calls=%async_computation.1 | async-start | bytes 2162688 | tf_op jit(solution)/shard_map/all_gather | solution.py:118
  10.3 516.5 %all-reduce.5.cloned.1.call-start = ((), (), s32[]{:S(2)}) async-start(), calls=%async_computation.2 | async-start | bytes 8388608
  176.2 7.6 %copy-start = (f32[2,4096,64,8]{1,2,3,0:T(8,128)}, f32[2,4096,64,8]{1,2,3,0:T(8,128)S(1)}, u32[]{:S(2)}) copy-start(f32[2,4096,64,8]{1,2,3,0:T(8,128)S(1)} %get-tuple-element.632) | copy-start | bytes 50331652 | tf_op jit(solution)/shard_map/cond
  176.8 6.9 %copy-start.11 = (bf16[4096,2,128]{2,0,1:T(8,128)(2,1)S(1)}, bf16[4096,2,128]{2,0,1:T(8,128)(2,1)}, u32[]{:S(2)}) copy-start(bf16[4096,2,128]{2,0,1:T(8,128)(2,1)} %get-tuple-element.421) | copy-start | bytes 6291460 | tf_op jit(solution)/shard_map/cond
  198.8 7.6 %copy-start.1 = (f32[2,4096,64,8]{1,2,3,0:T(8,128)}, f32[2,4096,64,8]{1,2,3,0:T(8,128)S(1)}, u32[]{:S(2)}) copy-start(f32[2,4096,64,8]{1,2,3,0:T(8,128)S(1)} %get-tuple-element.634) | copy-start | bytes 50331652 | tf_op jit(solution)/shard_map/cond
  199.5 6.9 %copy-start.12 = (bf16[4096,2,128]{2,0,1:T(8,128)(2,1)S(1)}, bf16[4096,2,128]{2,0,1:T(8,128)(2,1)}, u32[]{:S(2)}) copy-start(bf16[4096,2,128]{2,0,1:T(8,128)(2,1)} %get-tuple-element.428) | copy-start | bytes 6291460 | tf_op jit(solution)/shard_map/cond
  224.8 2.5 copy-start.2
  234.1 2.4 copy-start.4
  241.3 2.5 copy-start.2
  249.6 2.5 copy-start.2
  257.9 2.5 copy-start.2
  266.3 2.5 copy-start.2
  274.6 2.5 copy-start.2
  283.0 2.5 copy-start.2
  291.3 2.5 copy-start.2
  298.1 1.5 copy-start.17
  298.1 1.5 copy-start.19
  298.1 1.5 copy-start.21
  299.6 1.9 copy-start.5
  299.6 1.9 copy-start.6
  299.7 2.4 copy-start.9
  299.7 2.4 copy-start.10
  (72 other events, 79.5 us)
Sparse Core Ops, SparseCore 0:
  11.2 80.9 all-gather.2
  95.3 75.1 all-gather.4
  299.8 226.9 all-reduce.4
where the time goes:
time: 538 us; the launch traced here: 535 us
  waiting for transfers between devices  375 us (70%)
  other arithmetic  52.5 us (10%)
  local copies, waits for them, and re-layouts  45.9 us (9%)
  matrix products  33 us (6%)
  between operations  15.9 us (3%)
  loops' own time  12.5 us (2%)
    unnamed x4, waiting for transfers between devices  223 us
    all_gather x1, waiting for transfers between devices, on_device(): value_piece = lax.all_gather(values, 'ctx', axis=0, tiled=True)  78.4 us
    all_gather x1, waiting for transfers between devices, on_device(): key_piece = lax.all_gather(key_rows, 'ctx', axis=0, tiled=True)  74 us
    add x8, other arithmetic, backward_step(): grads_query[part_number] = grads_query[part_number] + query_part  17.7 us
    dot_general x2, matrix products, online_update(): jnp.einsum('agqk,kad->agqd', weights.astype(jnp.bfloat16), value_piece, p...  16.3 us
    reduce_sum x2, other arithmetic, online_update(): new_total = jnp.sum(weights, axis=-1)  13.8 us
    another operation x1, loops' own time, on_device(): lax.fori_loop(0, key_total // key_block_rows, backward_step, start_state)  11.6 us
  transfers between devices with their start and end apart: 3, of which 3 were waited for; matrix products, arithmetic and copies ran while one was open for 2% of the time, Pallas kernels for 0%

commit v1 on v0

v1 whole, which is shorter than its diff:
```python
import functools
import math

import jax
import jax.numpy as jnp
from jax import lax
from jax.experimental import pallas as pl
from jax.experimental.pallas import tpu as pltpu
from jax.sharding import PartitionSpec as P

MASKED_SCORE = -1e30
NY, NZ = 4, 8


def dot_tn(left, right):
    return lax.dot_general(left, right, (((0,), (0,)), ((), ())), preferred_element_type=jnp.float32)


def dot_nt(left, right, precision=None):
    return lax.dot_general(
        left, right, (((1,), (1,)), ((), ())), precision=precision, preferred_element_type=jnp.float32
    )


def dot_nn(left, right):
    return jnp.dot(left, right, preferred_element_type=jnp.float32)


def stage_kernel(stage, waits, block, group, *refs):
    offset, forward, finish, backward, last = stage
    first = forward and offset == 0
    paired = offset not in (0, 4)
    units = 4 if paired else 2
    lanes = block * group
    refs = list(refs)
    take = lambda count: [refs.pop(0) for _ in range(count)]
    take(waits)
    docs_ref, place_ref = take(2)
    q_in = take(2)
    g_in = take(2) if backward else []
    pieces = take(1 if offset == 0 else 2)
    state_in = take(3) if forward and not first else []
    stats_in = take(2) if backward and not finish else []
    dq_in = take(1) if backward and not finish else []
    state_out = take(3) if forward and not finish else []
    rows_out = take(2) if finish or last else []
    stats_out = take(2) if finish else []
    dq_out = take(1) if backward and not last else []
    grads = take(len(pieces)) if backward else []
    k_scr, v_scr, q_scr, s_scr, m_scr = take(5)
    if finish:
        state_out = take(3)
    if backward:
        g_scr, dk_scr, dv_scr = take(3)
    if last:
        dq_out = take(1)
    stats = stats_out or stats_in

    head_size = q_in[0].shape[1]
    scale = 1.0 / math.sqrt(head_size)
    log2_scale = scale * math.log2(math.e)
    y, z = place_ref[0], place_ref[1]

    def block_of(slot, distance):
        return lax.rem(y + NY - slot, NY) * NZ + lax.rem(z + NZ + distance, NZ)

    def blocks_of(unit):
        if paired:
            return block_of(unit, -offset), block_of(unit, offset)
        return block_of(2 * unit, offset), block_of(2 * unit + 1, offset)

    def places():
        for unit in range(units):
            for half in range(2):
                if paired:
                    yield unit, half, half, unit
                else:
                    yield unit, half, unit if offset else 0, half if offset else 2 * unit + half

    for unit, half, piece, slot in places():
        rows = pl.ds(half * block, block)
        k_scr[unit, rows, :] = pieces[piece][slot, 0]
        v_scr[unit, rows, :] = pieces[piece][slot, 1]
    for part in range(2):
        q_scr[part] = q_in[part][...]
        if backward:
            g_scr[part] = g_in[part][...]

    def doc_start(position):
        bound, start = jnp.int32(0), jnp.zeros_like(position)
        for number in range(docs_ref.shape[0]):
            bound = bound + docs_ref[number]
            start = jnp.where(bound <= position, bound, start)
        return start

    def fold(value):
        return value.reshape(value.shape[0] // 8, 8, value.shape[1])

    def part_facts(part):
        query_block = jnp.where(part == 0, y, NY - 1 - y) * NZ + z
        first_pos = query_block * block
        lane = lax.broadcasted_iota(jnp.int32, (1, lanes), 1)
        positions = first_pos + lane // group
        return query_block, positions, doc_start(positions), doc_start(first_pos), doc_start(first_pos + block - 1)

    def is_live(unit, facts):
        query_block, _, _, open_first, _ = facts
        one, two = ((n <= query_block) & ((n + 1) * block > open_first) for n in blocks_of(unit))
        return one | two

    def is_clear(unit, facts):
        query_block, _, _, _, open_last = facts
        one, two = ((n < query_block) & (n * block >= open_last) for n in blocks_of(unit))
        return one & two

    def scores_of(unit, part, facts, masked):
        scores = dot_nt(k_scr[unit], q_scr[part])
        if masked:
            _, positions, starts, _, _ = facts
            one, two = blocks_of(unit)
            row = lax.broadcasted_iota(jnp.int32, (2 * block, lanes), 0)
            key_pos = row + jnp.where(row < block, one, two - 1) * block
            scores = jnp.where((key_pos <= positions) & (key_pos >= starts), scores, MASKED_SCORE)
        return scores

    def each_unit(facts, work):
        def step(unit, _):
            live, clear = is_live(unit, facts), is_clear(unit, facts)
            pl.when(live & clear)(lambda: work(unit, False))
            pl.when(live & jnp.logical_not(clear))(lambda: work(unit, True))
            return 0

        lax.fori_loop(0, units, step, 0)

    def forward_part(part, _):
        facts = part_facts(part)
        m_new, l_new, o_new = state_out
        if first:
            m_old = jnp.full((8, lanes), MASKED_SCORE, jnp.float32)
        else:
            m_old = state_in[0][part]
        m_scr[...] = m_old

        def score(unit, masked):
            scores = scores_of(unit, part, facts, masked)
            s_scr[unit] = scores
            m_scr[...] = jnp.maximum(m_scr[...], jnp.max(fold(scores), axis=0))

        each_unit(facts, score)
        top = jnp.max(m_scr[...], axis=0, keepdims=True)
        m_new[part] = jnp.broadcast_to(top, (8, lanes))
        if first:
            l_new[part] = jnp.zeros((8, lanes), jnp.float32)
            o_new[part] = jnp.zeros((head_size, lanes), jnp.float32)
        else:
            fading = jnp.exp2((m_old - top) * log2_scale)
            l_new[part] = state_in[1][part] * fading
            o_new[part] = state_in[2][part] * fading[:1]
        row_max = top * log2_scale

        def weigh(unit, _):
            @pl.when(is_live(unit, facts))
            def _():
                weights = jnp.exp2(s_scr[unit] * log2_scale - row_max)
                l_new[part] += jnp.sum(fold(weights), axis=0)
                o_new[part] += dot_tn(v_scr[unit], weights.astype(jnp.bfloat16))

            return 0

        lax.fori_loop(0, units, weigh, 0)
        if finish:
            row_total = jnp.sum(l_new[part], axis=0, keepdims=True)
            attended = (o_new[part] / row_total).T.astype(jnp.bfloat16)
            products = attended.astype(jnp.float32) * g_scr[part].astype(jnp.float32)
            stats_out[0][part] = jnp.broadcast_to(row_max + jnp.log2(row_total), (8, lanes))
            stats_out[1][part] = dot_nt(jnp.ones((8, head_size), jnp.float32), products, lax.Precision.HIGHEST)
            write_rows(part, attended)
        return 0

    def write_rows(part, rows):
        for number in range(2):

            @pl.when(part == number)
            def _():
                rows_out[number][...] = rows

    def backward_part(part, _):
        facts = part_facts(part)
        log_total, out_dot = stats[0][part][:1], stats[1][part][:1]
        dq_new = dq_out[0]
        dq_new[part] = jnp.zeros((head_size, lanes), jnp.float32) if finish else dq_in[0][part]

        def differentiate(unit, masked):
            probs = jnp.exp2(scores_of(unit, part, facts, masked) * log2_scale - log_total)
            dprobs = dot_nt(v_scr[unit], g_scr[part])
            dscores = (probs * (dprobs - out_dot)).astype(jnp.bfloat16)
            dv_scr[unit] += dot_nn(probs.astype(jnp.bfloat16), g_scr[part])
            dk_scr[unit] += dot_nn(dscores, q_scr[part])
            dq_new[part] += dot_tn(k_scr[unit], dscores)

        each_unit(facts, differentiate)
        if last:
            write_rows(part, (dq_new[part] * scale).T.astype(jnp.bfloat16))
        return 0

    if forward:
        lax.fori_loop(0, 2, forward_part, 0)
    if backward:
        dk_scr[...] = jnp.zeros_like(dk_scr)
        dv_scr[...] = jnp.zeros_like(dv_scr)
        lax.fori_loop(0, 2, backward_part, 0)
        for unit, half, piece, slot in places():
            rows = pl.ds(half * block, block)
            grads[piece][slot, 0] = (dk_scr[unit, rows, :] * scale).astype(jnp.bfloat16)
            grads[piece][slot, 1] = dv_scr[unit, rows, :].astype(jnp.bfloat16)


def run_stage(stage, block, group, facts, q_parts, g_parts, pieces, state=(), stats=(), dq=(), after=()):
    offset, forward, finish, backward, last = stage
    units = 2 if offset in (0, 4) else 4
    lanes, head_size = q_parts[0].shape
    f32 = lambda *shape: jax.ShapeDtypeStruct(shape, jnp.float32)
    low = lambda array: jax.ShapeDtypeStruct(array.shape, jnp.bfloat16)
    state_shapes = [f32(2, 8, lanes), f32(2, 8, lanes), f32(2, head_size, lanes)]
    dq_shape = f32(2, head_size, lanes)
    operands = [*after, *facts, *q_parts, *(g_parts if backward else ()), *pieces, *state, *stats, *dq]
    outs = []
    aliases = {}
    if forward and not finish:
        if state:
            aliases = {len(operands) - 3 + n: n for n in range(3)}
        outs += state_shapes
    if finish or last:
        outs += [low(q) for q in q_parts]
    if finish:
        outs += state_shapes[:2]
    if backward and not last:
        if dq:
            aliases = {len(operands) - 1: len(outs)}
        outs += [dq_shape]
    if backward:
        outs += [low(piece) for piece in pieces]
    scratch = [
        pltpu.VMEM((units, 2 * block, head_size), jnp.bfloat16),
        pltpu.VMEM((units, 2 * block, head_size), jnp.bfloat16),
        pltpu.VMEM((2, lanes, head_size), jnp.bfloat16),
        pltpu.VMEM((units if forward else 1, 2 * block, lanes), jnp.float32),
        pltpu.VMEM((8, lanes), jnp.float32),
    ]
    if finish:
        scratch += [pltpu.VMEM(shape.shape, jnp.float32) for shape in state_shapes]
    if backward:
        scratch += [
            pltpu.VMEM((2, lanes, head_size), jnp.bfloat16),
            pltpu.VMEM((units, 2 * block, head_size), jnp.float32),
            pltpu.VMEM((units, 2 * block, head_size), jnp.float32),
        ]
    if last:
        scratch += [pltpu.VMEM(dq_shape.shape, jnp.float32)]
    smem = pl.BlockSpec(memory_space=pltpu.SMEM)
    vmem = pl.BlockSpec(memory_space=pltpu.VMEM)
    products = 2 * forward + 5 * backward
    return pl.pallas_call(
        functools.partial(stage_kernel, stage, len(after), block, group),
        out_shape=outs,
        in_specs=[pl.BlockSpec(memory_space=pl.ANY)] * len(after) + [smem, smem] + [vmem] * (len(operands) - 2 - len(after)),
        out_specs=[vmem] * len(outs),
        scratch_shapes=scratch,
        input_output_aliases=aliases,
        compiler_params=pltpu.CompilerParams(vmem_limit_bytes=24 * 1024 * 1024),
        cost_estimate=pl.CostEstimate(
            flops=6 * products * 2 * lanes * units * 2 * block * head_size,
            bytes_accessed=4 * 1024 * 1024,
            transcendentals=2 * lanes * units * 2 * block,
        ),
        name="fwd" * forward + "bwd" * backward + str(offset),
    )(*operands)


def y_turn(turn):
    return [(y * NZ + z, ((y + turn) % NY) * NZ + z) for y in range(NY) for z in range(NZ)]


def z_turn(turn):
    return [(y * NZ + z, y * NZ + (z + turn) % NZ) for y in range(NY) for z in range(NZ)]


MIRROR = [(y * NZ + z, (NY - 1 - y) * NZ + z) for y in range(NY) for z in range(NZ)]


def add_up(one, other):
    return (one.astype(jnp.float32) + other.astype(jnp.float32)).astype(jnp.bfloat16)


def move_right(array):
    return lax.ppermute(array, "ctx", z_turn(1))


def move_left(array):
    return lax.ppermute(array, "ctx", z_turn(-1))


def on_device(queries, key_rows, values, out_grad, doc_lengths):
    block, query_heads, head_size = queries.shape
    key_heads = key_rows.shape[1]
    group = query_heads // key_heads
    place = lax.axis_index("ctx")
    y, z = place // NZ, place % NZ
    mine = y // 2

    def head_of(array, number, width):
        picked = jnp.where(number == 0, array[:, :width], array[:, width:])
        return picked.reshape(block * width, head_size)

    def key_pair(number):
        return jnp.stack([head_of(key_rows, number, 1), head_of(values, number, 1)])

    held = [key_pair(mine)]
    for turn in range(1, NY):
        held.append(lax.ppermute(key_pair(((y + turn) % NY) // 2), "ctx", y_turn(turn)))
    column = jnp.stack(held)

    def both_rows(array):
        return [head_of(array, mine, group), lax.ppermute(head_of(array, 1 - mine, group), "ctx", MIRROR)]

    q_parts, g_parts = both_rows(queries), both_rows(out_grad)
    facts = (doc_lengths, jnp.stack([y, z]).astype(jnp.int32))
    run = functools.partial(run_stage, block=block, group=group, facts=facts, q_parts=q_parts, g_parts=g_parts)

    right, left = [column], [column]
    state = ()
    for step in range(4):
        pieces = [column] if step == 0 else [right[step], left[step]]
        if step < 3:
            right.append(move_right(right[step]))
            left.append(move_left(left[step]))
        else:
            right.append(move_right(right[step][:2]))
            left.append(move_left(left[step][2:]))
        state = run((step, True, False, False, False), pieces=pieces, state=state)
    own_out, other_out, log_total, out_dot, dq, from_right, from_left = run(
        (4, True, True, True, False), pieces=[right[4], left[4]], state=state
    )
    stats = (log_total, out_dot)
    other_out = lax.ppermute(other_out, "ctx", MIRROR)
    from_right, from_left = move_right(from_right), move_left(from_left)
    after = ()
    for step in (3, 2, 1):
        dq, behind, ahead = run(
            (step, False, False, True, False), pieces=[right[step], left[step]], stats=stats, dq=(dq,), after=after
        )
        arrived_right, arrived_left = from_right, from_left
        if step == 3:
            from_right = jnp.concatenate([add_up(ahead[:2], from_right), ahead[2:]], axis=0)
            from_left = jnp.concatenate([behind[:2], add_up(behind[2:], from_left)], axis=0)
        else:
            from_right, from_left = add_up(ahead, from_right), add_up(behind, from_left)
        after = (arrived_right, arrived_left)
        from_right, from_left = move_right(from_right), move_left(from_left)
    own_dq, other_dq, grad = run((0, False, False, True, True), pieces=[column], stats=stats, dq=(dq,), after=after)
    other_dq = lax.ppermute(other_dq, "ctx", MIRROR)
    sums = grad.astype(jnp.float32) + from_right.astype(jnp.float32) + from_left.astype(jnp.float32)

    def both_heads(own, other):
        one, two = (r.reshape(block, group, head_size) for r in (own, other))
        return jnp.concatenate([jnp.where(mine == 0, one, two), jnp.where(mine == 0, two, one)], axis=1)

    attended, query_grad = both_heads(own_out, other_out), both_heads(own_dq, other_dq)
    terms = [(mine, sums[0])]
    for turn in range(1, NY):
        arrived = lax.ppermute(sums[turn].astype(jnp.bfloat16), "ctx", y_turn(-turn)).astype(jnp.float32)
        terms.append((((y + turn) % NY) // 2, arrived))
    heads = [sum(jnp.where(number == head, term, 0.0) for number, term in terms) for head in range(2)]
    grads = jnp.stack(heads, axis=2).astype(jnp.bfloat16)
    return attended, query_grad, grads[0], grads[1]


def solution(mesh):
    placed = (
        P(("dp", "ctx"), "head", None),
        P(("dp", "ctx"), "head", None),
        P(("dp", "ctx"), "head", None),
        P(("dp", "ctx"), "head", None),
        P("dp"),
    )
    return jax.shard_map(
        on_device,
        mesh=mesh,
        in_specs=placed,
        out_specs=(
            P(("dp", "ctx"), "head", None),
            P(("dp", "ctx"), "head", None),
            P(("dp", "ctx"), "head", None),
            P(("dp", "ctx"), "head", None),
        ),
        check_vma=False,
    )
```

time: 538 us -> 104 us (0.19)
  waiting for transfers between devices: 375 us -> 13.2 us
  starting transfers between devices: 0.12 us -> 49.9 us
  other arithmetic: 52.5 us -> 2.76 us
  local copies, waits for them, and re-layouts: 45.9 us -> 3.78 us
  matrix products: 33 us -> 0 us
  Pallas kernels: 0 us -> 31.7 us
  between operations: 15.9 us -> 1.16 us
  loops' own time: 12.5 us -> 0 us
    unnamed x4 -> x0, waiting for transfers between devices: 223 us -> none
    all_gather x2 -> x0, waiting for transfers between devices: 152 us -> none  [the longest x1 78.4 us: on_device(): value_piece = lax.all_gather(values, 'ctx', axis=0, tiled=True)]
    ppermute x0 -> x26, starting transfers between devices: none -> 49.9 us  [the longest x8 30.5 us: move_left(): return lax.ppermute(array, 'ctx', z_turn(-1))]
    dot_general x14 -> x0, matrix products: 33 us -> none  [the longest x2 16.3 us: online_update(): jnp.einsum('agqk,kad->agqd', weights.astype(jnp.bfloat16), value_piece, p...]
    pallas_call x0 -> x9, Pallas kernels: none -> 31.7 us  [run_stage(): pl.pallas_call(functools.partial(stage_kernel, stage, len(after), block,...]
    reduce_sum x14 -> x0, other arithmetic: 24.6 us -> none  [the longest x2 13.8 us: online_update(): new_total = jnp.sum(weights, axis=-1)]
    add x35 -> x0, other arithmetic: 21.2 us -> none  [the longest x8 17.7 us: backward_step(): grads_query[part_number] = grads_query[part_number] + query_part]
    dynamic_slice x16 -> x0, local copies, waits for them, and re-layouts: 15.7 us -> none  [the longest x8 7.84 us: backward_step(): lax.dynamic_slice_in_dim(whole_values, key_start, key_block_rows, 0)]
  transfers between devices with their start and end apart: 3 -> 26, of which waited for: 3 -> 10; matrix products, arithmetic and copies ran while one was open for 2% -> 3% of each run, Pallas kernels for 0% -> 27%
where the time goes in v1:
time: 104 us; the launch traced here: 103 us
  starting transfers between devices  49.9 us (48%)
  Pallas kernels  31.7 us (30%)
  waiting for transfers between devices  13.2 us (13%)
  local copies, waits for them, and re-layouts  3.78 us (4%)
  other arithmetic  2.76 us (3%)
  between operations  1.16 us (1%)
    pallas_call x9, Pallas kernels, run_stage(): pl.pallas_call(functools.partial(stage_kernel, stage, len(after), block,...  31.7 us
    ppermute x8, starting transfers between devices, move_left(): return lax.ppermute(array, 'ctx', z_turn(-1))  30.5 us
    ppermute x8, waiting for transfers between devices, move_right(): return lax.ppermute(array, 'ctx', z_turn(1))  5.52 us
    ppermute x1, starting transfers between devices, on_device(): other_out = lax.ppermute(other_out, 'ctx', MIRROR)  5.44 us
    ppermute x3, starting transfers between devices, on_device(): lax.ppermute(key_pair((y + turn) % NY // 2), 'ctx', y_turn(turn))  4.85 us
    ppermute x3, starting transfers between devices, on_device(): lax.ppermute(sums[turn].astype(jnp.bfloat16), 'ctx', y_turn(-turn))  3.99 us
    unnamed x12, local copies, waits for them, and re-layouts  3.53 us
    ppermute x2, starting transfers between devices, both_rows(): lax.ppermute(head_of(array, 1 - mine, group), 'ctx', MIRROR)  3.41 us
  transfers between devices with their start and end apart: 26, of which 10 were waited for; matrix products, arithmetic and copies ran while one was open for 3% of the time, Pallas kernels for 27%

profile of v1, /device:TPU:6, one launch (start us, length us, event | category | flops | bytes accessed | tf_op | source)
XLA Modules:
  0.0 102.6 jit_solution(9908383951426540844)
XLA Ops:
  2.6 3.1 %collective-permute-start.4 = (bf16[2,128,128]{2,1,0:T(8,128)(2,1)S(1)}, bf16[2,128,128]{2,1,0:T(8,128)(2,1)S(1)}, u32[]{:S(2)}, u32[]{:S(2)}) collective-permute-start(bf16[2,128,128]{2,1,0:T(8,128)(2,1)S(1)} %pad_maximum_fusion.8), channel_id=1, source_target_pairs={{0,48},{2,50},{4,52},{6,54},{8,56},{10,58},{12,60},{14,62},{16,0},... | collective-permute-start | bytes 196616 | tf_op jit(solution)/shard_map/ppermute | solution.py:320
  7.5 2.4 %collective-permute-start = (bf16[1024,128]{1,0:T(8,128)(2,1)S(1)}, bf16[1024,128]{1,0:T(8,128)(2,1)S(1)}, u32[]{:S(2)}, u32[]{:S(2)}) collective-permute-start(bf16[1024,128]{1,0:T(8,128)(2,1)S(1)} %get-tuple-element.86), channel_id=1, source_target_pairs={{0,48},{2,50},{4,52},{6,54},{8,56},{10,58},{12,60},{14,62},{16,32}... | collective-permute-start | bytes 786440 | tf_op jit(solution)/shard_map/ppermute | solution.py:324
  13.1 5.9 %collective-permute-start.9 = (bf16[4,2,128,128]{3,2,1,0:T(8,128)(2,1)S(1)}, bf16[4,2,128,128]{3,2,1,0:T(8,128)(2,1)S(1)}, u32[]{:S(2)}, u32[]{:S(2)}) collective-permute-start(bf16[4,2,128,128]{3,2,1,0:T(8,128)(2,1)S(1)} %pad_maximum_fusion.2.refs_4_.refs_8_), channel_id=1, source_target_pairs={{0,14},{2,0},{4,2},{6,4},{8,6},{10,8},{12,10},{14,12},{16,30},{18,... | collective-permute-start | bytes 786440 | tf_op jit(solution)/shard_map/ppermute | solution.py:300
  19.7 2.9 %fwd0.1 = (f32[2,8,1024]{2,1,0:T(8,128)S(1)}, f32[2,8,1024]{2,1,0:T(8,128)S(1)}, f32[2,128,1024]{2,1,0:T(8,128)S(1)}) custom-call(s32[16]{0:T(128)S(1)} %copy-done, s32[2]{0:T(128)S(1)} %pad_add_fusion.refs_1_.refs_3_, bf16[1024,128]{1,0:T(8,128)(2,1)S(1)} %get-tuple-element.87.refs_2_.refs_4_, bf16[1024,128]{1,0:T(8,128)(2,1)S(1)} %collective-permute-done.refs_3_.refs_5_, ...), custom_call_target="tpu_custom_call" | custom-call | flops 1610612736 | bytes 4194304 | tf_op jit(solution)/shard_map/fwd0/pallas_call | solution.py:263
  22.9 4.0 %collective-permute-start.10 = (bf16[4,2,128,128]{3,2,1,0:T(8,128)(2,1)S(1)}, bf16[4,2,128,128]{3,2,1,0:T(8,128)(2,1)S(1)}, u32[]{:S(2)}, u32[]{:S(2)}) collective-permute-start(bf16[4,2,128,128]{3,2,1,0:T(8,128)(2,1)S(1)} %collective-permute-done.9.refs_5_.refs_9_), channel_id=1, source_target_pairs={{0,14},{2,0},{4,2},{6,4},{8,6},{10,8},{12,10},{14,12},{16,30},{18,... | collective-permute-start | bytes 786440 | tf_op jit(solution)/shard_map/ppermute | solution.py:300
  26.9 3.2 %fwd1.1 = (f32[2,8,1024]{2,1,0:T(8,128)S(1)}, f32[2,8,1024]{2,1,0:T(8,128)S(1)}, f32[2,128,1024]{2,1,0:T(8,128)S(1)}) custom-call(s32[16]{0:T(128)S(1)} %copy-done, s32[2]{0:T(128)S(1)} %pad_add_fusion.refs_1_.refs_3_, bf16[1024,128]{1,0:T(8,128)(2,1)S(1)} %get-tuple-element.87.refs_2_.refs_4_, ...), custom_call_target="tpu_custom_call", output_to_operand_aliasing={{0}: (6, {}), {1}: (7, {}), {2}: (8, {})} | custom-call | flops 3221225472 | bytes 4194304 | tf_op jit(solution)/shard_map/fwd1/pallas_call | solution.py:263
  31.1 3.7 %collective-permute-start.11 = (bf16[4,2,128,128]{3,2,1,0:T(8,128)(2,1)S(1)}, bf16[4,2,128,128]{3,2,1,0:T(8,128)(2,1)S(1)}, u32[]{:S(2)}, u32[]{:S(2)}) collective-permute-start(bf16[4,2,128,128]{3,2,1,0:T(8,128)(2,1)S(1)} %collective-permute-done.10.refs_5_.refs_9_), channel_id=1, source_target_pairs={{0,14},{2,0},{4,2},{6,4},{8,6},{10,8},{12,10},{14,12},{16,30},{18,... | collective-permute-start | bytes 786440 | tf_op jit(solution)/shard_map/ppermute | solution.py:300
  34.8 3.2 %fwd2.1 = (f32[2,8,1024]{2,1,0:T(8,128)S(1)}, f32[2,8,1024]{2,1,0:T(8,128)S(1)}, f32[2,128,1024]{2,1,0:T(8,128)S(1)}) custom-call(s32[16]{0:T(128)S(1)} %copy-done, s32[2]{0:T(128)S(1)} %pad_add_fusion.refs_1_.refs_3_, bf16[1024,128]{1,0:T(8,128)(2,1)S(1)} %get-tuple-element.87.refs_2_.refs_4_, ...), custom_call_target="tpu_custom_call", output_to_operand_aliasing={{0}: (6, {}), {1}: (7, {}), {2}: (8, {})} | custom-call | flops 3221225472 | bytes 4194304 | tf_op jit(solution)/shard_map/fwd2/pallas_call | solution.py:263
  38.7 3.9 %collective-permute-start.12 = (bf16[2,2,128,128]{3,2,1,0:T(8,128)(2,1)S(1)}, bf16[2,2,128,128]{3,2,1,0:T(8,128)(2,1)S(1)}, u32[]{:S(2)}, u32[]{:S(2)}) collective-permute-start(bf16[2,2,128,128]{3,2,1,0:T(8,128)(2,1)S(1)} %slice.100), channel_id=1, source_target_pairs={{0,14},{2,0},{4,2},{6,4},{8,6},{10,8},{12,10},{14,12},{16,30},{18,... | collective-permute-start | bytes 393224 | tf_op jit(solution)/shard_map/ppermute | solution.py:300
  42.8 3.2 %fwd3.1 = (f32[2,8,1024]{2,1,0:T(8,128)S(1)}, f32[2,8,1024]{2,1,0:T(8,128)S(1)}, f32[2,128,1024]{2,1,0:T(8,128)S(1)}) custom-call(s32[16]{0:T(128)S(1)} %copy-done, s32[2]{0:T(128)S(1)} %pad_add_fusion.refs_1_.refs_3_, bf16[1024,128]{1,0:T(8,128)(2,1)S(1)} %get-tuple-element.87.refs_2_.refs_4_, ...), custom_call_target="tpu_custom_call", output_to_operand_aliasing={{0}: (6, {}), {1}: (7, {}), {2}: (8, {})} | custom-call | flops 3221225472 | bytes 4194304 | tf_op jit(solution)/shard_map/fwd3/pallas_call | solution.py:263
  46.0 2.9 %collective-permute-done.8.refs_6_ = bf16[2,2,128,128]{3,2,1,0:T(8,128)(2,1)S(1)} collective-permute-done((bf16[2,2,128,128]{3,2,1,0:T(8,128)(2,1)S(1)}, bf16[2,2,128,128]{3,2,1,0:T(8,128)(2,1)S(1)}, u32[]{:S(2)}, u32[]{:S(2)}) %collective-permute-start.8) | collective-permute-done | bytes 131104 | tf_op jit(solution)/shard_map/ppermute | solution.py:296
  48.9 4.0 %fwdbwd4.1 = (bf16[1024,128]{1,0:T(8,128)(2,1)S(1)}, bf16[1024,128]{1,0:T(8,128)(2,1)S(1)}, f32[2,8,1024]{2,1,0:T(8,128)S(1)}, f32[2,8,1024]{2,1,0:T(8,128)S(1)}...) custom-call(s32[16]{0:T(128)S(1)} %copy-done, ...), custom_call_target="tpu_custom_call" | custom-call | flops 5637144576 | bytes 4194304 | tf_op jit(solution)/shard_map/fwdbwd4/pallas_call | solution.py:263
  53.5 2.8 %collective-permute-start.15 = (bf16[2,2,128,128]{3,2,1,0:T(8,128)(2,1)S(1)}, bf16[2,2,128,128]{3,2,1,0:T(8,128)(2,1)S(1)}, u32[]{:S(2)}, u32[]{:S(2)}) collective-permute-start(bf16[2,2,128,128]{3,2,1,0:T(8,128)(2,1)S(1)} %get-tuple-element.50), channel_id=1, source_target_pairs={{0,14},{2,0},{4,2},{6,4},{8,6},{10,8},{12,10},{14,12},{16,30},{18,... | collective-permute-start | bytes 393224 | tf_op jit(solution)/shard_map/ppermute | solution.py:300
  56.3 5.4 %collective-permute-start.13 = (bf16[1024,128]{1,0:T(8,128)(2,1)S(1)}, bf16[1024,128]{1,0:T(8,128)(2,1)S(1)}, u32[]{:S(2)}, u32[]{:S(2)}) collective-permute-start(bf16[1024,128]{1,0:T(8,128)(2,1)S(1)} %get-tuple-element.48), channel_id=1, source_target_pairs={{0,48},{2,50},{4,52},{6,54},{8,56},{10,58},{12,60},{14,62},{16,32}... | collective-permute-start | bytes 786440 | tf_op jit(solution)/shard_map/ppermute | solution.py:345
  61.7 3.7 %bwd3.1 = (f32[2,128,1024]{2,1,0:T(8,128)S(1)}, bf16[4,2,128,128]{3,2,1,0:T(8,128)(2,1)S(1)}, bf16[4,2,128,128]{3,2,1,0:T(8,128)(2,1)S(1)}) custom-call(s32[16]{0:T(128)S(1)} %copy-done, s32[2]{0:T(128)S(1)} %pad_add_fusion.refs_1_.refs_3_, bf16[1024,128]{1,0:T(8,128)(2,1)S(1)} %get-tuple-element.87.refs_2_.refs_4_, ...), custom_call_target="tpu_custom_call", output_to_operand_aliasing={{0}: (10, {})} | custom-call | flops 8053063680 | bytes 4194304 | tf_op jit(solution)/shard_map/bwd3/pallas_call | solution.py:263
  65.8 3.5 %collective-permute-start.18 = (bf16[4,2,128,128]{3,2,1,0:T(8,128)(2,1)S(1)}, bf16[4,2,128,128]{3,2,1,0:T(8,128)(2,1)S(1)}, u32[]{:S(2)}, u32[]{:S(2)}) collective-permute-start(bf16[4,2,128,128]{3,2,1,0:T(8,128)(2,1)S(1)} %pad_maximum_fusion.4), channel_id=1, source_target_pairs={{0,14},{2,0},{4,2},{6,4},{8,6},{10,8},{12,10},{14,12},{16,30},{18,... | collective-permute-start | bytes 786440 | tf_op jit(solution)/shard_map/ppermute | solution.py:300
  69.3 3.7 %bwd2.1 = (f32[2,128,1024]{2,1,0:T(8,128)S(1)}, bf16[4,2,128,128]{3,2,1,0:T(8,128)(2,1)S(1)}, bf16[4,2,128,128]{3,2,1,0:T(8,128)(2,1)S(1)}) custom-call(bf16[2,2,128,128]{3,2,1,0:T(8,128)(2,1)S(1)} %collective-permute-done.14.refs_0_, bf16[2,2,128,128]{3,2,1,0:T(8,128)(2,1)S(1)} %collective-permute-done.15.refs_1_, ...), custom_call_target="tpu_custom_call", output_to_operand_aliasing={{0}: (12, {})} | custom-call | flops 8053063680 | bytes 4194304 | tf_op jit(solution)/shard_map/bwd2/pallas_call | solution.py:263
  75.4 3.3 %collective-permute-start.19 = (bf16[4,2,128,128]{3,2,1,0:T(8,128)(2,1)S(1)}, bf16[4,2,128,128]{3,2,1,0:T(8,128)(2,1)S(1)}, u32[]{:S(2)}, u32[]{:S(2)}) collective-permute-start(bf16[4,2,128,128]{3,2,1,0:T(8,128)(2,1)S(1)} %add_convert_fusion.2), channel_id=1, source_target_pairs={{0,14},{2,0},{4,2},{6,4},{8,6},{10,8},{12,10},{14,12},{16,30},{18,... | collective-permute-start | bytes 786440 | tf_op jit(solution)/shard_map/ppermute | solution.py:300
  78.6 3.7 %bwd1.1 = (f32[2,128,1024]{2,1,0:T(8,128)S(1)}, bf16[4,2,128,128]{3,2,1,0:T(8,128)(2,1)S(1)}, bf16[4,2,128,128]{3,2,1,0:T(8,128)(2,1)S(1)}) custom-call(bf16[4,2,128,128]{3,2,1,0:T(8,128)(2,1)S(1)} %collective-permute-done.16.refs_0_, bf16[4,2,128,128]{3,2,1,0:T(8,128)(2,1)S(1)} %collective-permute-done.18.refs_1_, ...), custom_call_target="tpu_custom_call", output_to_operand_aliasing={{0}: (12, {})} | custom-call | flops 8053063680 | bytes 4194304 | tf_op jit(solution)/shard_map/bwd1/pallas_call | solution.py:263
  84.1 3.3 %collective-permute-start.22 = (bf16[4,2,128,128]{3,2,1,0:T(8,128)(2,1)S(1)}, bf16[4,2,128,128]{3,2,1,0:T(8,128)(2,1)S(1)}, u32[]{:S(2)}, u32[]{:S(2)}) collective-permute-start(bf16[4,2,128,128]{3,2,1,0:T(8,128)(2,1)S(1)} %add_convert_fusion), channel_id=1, source_target_pairs={{0,14},{2,0},{4,2},{6,4},{8,6},{10,8},{12,10},{14,12},{16,30},{18,... | collective-permute-start | bytes 786440 | tf_op jit(solution)/shard_map/ppermute | solution.py:300
  87.4 4.0 %bwd0.1 = (bf16[1024,128]{1,0:T(8,128)(2,1)S(1)}, bf16[1024,128]{1,0:T(8,128)(2,1)S(1)}, bf16[4,2,128,128]{3,2,1,0:T(8,128)(2,1)S(1)}) custom-call(bf16[4,2,128,128]{3,2,1,0:T(8,128)(2,1)S(1)} %collective-permute-done.17.refs_0_, bf16[4,2,128,128]{3,2,1,0:T(8,128)(2,1)S(1)} %collective-permute-done.19.refs_1_, s32[16]{0:T(128)S(1)} %copy-done, ...), custom_call_target="tpu_custom_call" | custom-call | flops 4026531840 | bytes 4194304 | tf_op jit(solution)/shard_map/bwd0/pallas_call | solution.py:263
  92.5 2.4 %collective-permute-start.23 = (bf16[2,128,128]{2,1,0:T(8,128)(2,1)S(1)}, bf16[2,128,128]{2,1,0:T(8,128)(2,1)S(1)}, u32[]{:S(2)}, u32[]{:S(2)}) collective-permute-start(bf16[2,128,128]{2,1,0:T(8,128)(2,1)S(1)} %get-tuple-element.88), channel_id=1, source_target_pairs={{0,48},{2,50},{4,52},{6,54},{8,56},{10,58},{12,60},{14,62},{16,0},... | collective-permute-start | bytes 196616 | tf_op jit(solution)/shard_map/ppermute | solution.py:371
  94.9 1.6 %collective-permute-start.24 = (bf16[2,128,128]{2,1,0:T(8,128)(2,1)S(1)}, bf16[2,128,128]{2,1,0:T(8,128)(2,1)S(1)}, u32[]{:S(2)}, u32[]{:S(2)}) collective-permute-start(bf16[2,128,128]{2,1,0:T(8,128)(2,1)S(1)} %get-tuple-element.90), channel_id=1, source_target_pairs={{0,32},{2,34},{4,36},{6,38},{8,40},{10,42},{12,44},{14,46},{16,48}... | collective-permute-start | bytes 196616 | tf_op jit(solution)/shard_map/ppermute | solution.py:371
  96.4 2.6 %collective-permute-done.20 = bf16[1024,128]{1,0:T(8,128)(2,1)S(1)} collective-permute-done((bf16[1024,128]{1,0:T(8,128)(2,1)S(1)}, bf16[1024,128]{1,0:T(8,128)(2,1)S(1)}, u32[]{:S(2)}, u32[]{:S(2)}) %collective-permute-start.20) | collective-permute-done | bytes 262176 | tf_op jit(solution)/shard_map/ppermute | solution.py:361
  (82 shorter events, 18.9 us)
Async XLA Ops:
  2.6 8.4 %collective-permute-start.4 = (bf16[2,128,128]{2,1,0:T(8,128)(2,1)S(1)}, bf16[2,128,128]{2,1,0:T(8,128)(2,1)S(1)}, u32[]{:S(2)}, u32[]{:S(2)}) collective-permute-start(bf16[2,128,128]{2,1,0:T(8,128)(2,1)S(1)} %pad_maximum_fusion.8), channel_id=1, source_target_pairs={{0,48},{2,50},{4,52},{6,54},{8,56},{10,58},{12,60},{14,62},{16,0},... | collective-permute-start | bytes 196616 | tf_op jit(solution)/shard_map/ppermute | solution.py:320
  6.4 6.6 %collective-permute-start.2 = (bf16[2,128,128]{2,1,0:T(8,128)(2,1)S(1)}, bf16[2,128,128]{2,1,0:T(8,128)(2,1)S(1)}, u32[]{:S(2)}, u32[]{:S(2)}) collective-permute-start(bf16[2,128,128]{2,1,0:T(8,128)(2,1)S(1)} %pad_maximum_fusion.6), channel_id=1, source_target_pairs={{0,16},{2,18},{4,20},{6,22},{8,24},{10,26},{12,28},{14,30},{16,32}... | collective-permute-start | bytes 196616 | tf_op jit(solution)/shard_map/ppermute | solution.py:320
  7.5 11.6 %collective-permute-start = (bf16[1024,128]{1,0:T(8,128)(2,1)S(1)}, bf16[1024,128]{1,0:T(8,128)(2,1)S(1)}, u32[]{:S(2)}, u32[]{:S(2)}) collective-permute-start(bf16[1024,128]{1,0:T(8,128)(2,1)S(1)} %get-tuple-element.86), channel_id=1, source_target_pairs={{0,48},{2,50},{4,52},{6,54},{8,56},{10,58},{12,60},{14,62},{16,32}... | collective-permute-start | bytes 786440 | tf_op jit(solution)/shard_map/ppermute | solution.py:324
  9.9 36.1 %collective-permute-start.1 = (bf16[1024,128]{1,0:T(8,128)(2,1)S(1)}, bf16[1024,128]{1,0:T(8,128)(2,1)S(1)}, u32[]{:S(2)}, u32[]{:S(2)}) collective-permute-start(bf16[1024,128]{1,0:T(8,128)(2,1)S(1)} %get-tuple-element.84), channel_id=1, source_target_pairs={{0,48},{2,50},{4,52},{6,54},{8,56},{10,58},{12,60},{14,62},{16,32}... | collective-permute-start | bytes 786440 | tf_op jit(solution)/shard_map/ppermute | solution.py:324
  13.1 9.8 %collective-permute-start.9 = (bf16[4,2,128,128]{3,2,1,0:T(8,128)(2,1)S(1)}, bf16[4,2,128,128]{3,2,1,0:T(8,128)(2,1)S(1)}, u32[]{:S(2)}, u32[]{:S(2)}) collective-permute-start(bf16[4,2,128,128]{3,2,1,0:T(8,128)(2,1)S(1)} %pad_maximum_fusion.2.refs_4_.refs_8_), channel_id=1, source_target_pairs={{0,14},{2,0},{4,2},{6,4},{8,6},{10,8},{12,10},{14,12},{16,30},{18,... | collective-permute-start | bytes 786440 | tf_op jit(solution)/shard_map/ppermute | solution.py:300
  19.0 7.9 %collective-permute-start.5 = (bf16[4,2,128,128]{3,2,1,0:T(8,128)(2,1)S(1)}, bf16[4,2,128,128]{3,2,1,0:T(8,128)(2,1)S(1)}, u32[]{:S(2)}, u32[]{:S(2)}) collective-permute-start(bf16[4,2,128,128]{3,2,1,0:T(8,128)(2,1)S(1)} %pad_maximum_fusion.2.refs_4_.refs_8_), channel_id=1, source_target_pairs={{0,2},{2,4},{4,6},{6,8},{8,10},{10,12},{12,14},{14,0},{16,18},{18,... | collective-permute-start | bytes 786440 | tf_op jit(solution)/shard_map/ppermute | solution.py:296
  22.9 8.2 %collective-permute-start.10 = (bf16[4,2,128,128]{3,2,1,0:T(8,128)(2,1)S(1)}, bf16[4,2,128,128]{3,2,1,0:T(8,128)(2,1)S(1)}, u32[]{:S(2)}, u32[]{:S(2)}) collective-permute-start(bf16[4,2,128,128]{3,2,1,0:T(8,128)(2,1)S(1)} %collective-permute-done.9.refs_5_.refs_9_), channel_id=1, source_target_pairs={{0,14},{2,0},{4,2},{6,4},{8,6},{10,8},{12,10},{14,12},{16,30},{18,... | collective-permute-start | bytes 786440 | tf_op jit(solution)/shard_map/ppermute | solution.py:300
  26.9 7.9 %collective-permute-start.6 = (bf16[4,2,128,128]{3,2,1,0:T(8,128)(2,1)S(1)}, bf16[4,2,128,128]{3,2,1,0:T(8,128)(2,1)S(1)}, u32[]{:S(2)}, u32[]{:S(2)}) collective-permute-start(bf16[4,2,128,128]{3,2,1,0:T(8,128)(2,1)S(1)} %collective-permute-done.5.refs_4_.refs_8_), channel_id=1, source_target_pairs={{0,2},{2,4},{4,6},{6,8},{8,10},{10,12},{12,14},{14,0},{16,18},{18,... | collective-permute-start | bytes 786440 | tf_op jit(solution)/shard_map/ppermute | solution.py:296
  31.1 7.6 %collective-permute-start.11 = (bf16[4,2,128,128]{3,2,1,0:T(8,128)(2,1)S(1)}, bf16[4,2,128,128]{3,2,1,0:T(8,128)(2,1)S(1)}, u32[]{:S(2)}, u32[]{:S(2)}) collective-permute-start(bf16[4,2,128,128]{3,2,1,0:T(8,128)(2,1)S(1)} %collective-permute-done.10.refs_5_.refs_9_), channel_id=1, source_target_pairs={{0,14},{2,0},{4,2},{6,4},{8,6},{10,8},{12,10},{14,12},{16,30},{18,... | collective-permute-start | bytes 786440 | tf_op jit(solution)/shard_map/ppermute | solution.py:300
  34.8 7.9 %collective-permute-start.7 = (bf16[4,2,128,128]{3,2,1,0:T(8,128)(2,1)S(1)}, bf16[4,2,128,128]{3,2,1,0:T(8,128)(2,1)S(1)}, u32[]{:S(2)}, u32[]{:S(2)}) collective-permute-start(bf16[4,2,128,128]{3,2,1,0:T(8,128)(2,1)S(1)} %collective-permute-done.6.refs_4_.refs_8_), channel_id=1, source_target_pairs={{0,2},{2,4},{4,6},{6,8},{8,10},{10,12},{12,14},{14,0},{16,18},{18,... | collective-permute-start | bytes 786440 | tf_op jit(solution)/shard_map/ppermute | solution.py:296
  38.7 7.3 %collective-permute-start.12 = (bf16[2,2,128,128]{3,2,1,0:T(8,128)(2,1)S(1)}, bf16[2,2,128,128]{3,2,1,0:T(8,128)(2,1)S(1)}, u32[]{:S(2)}, u32[]{:S(2)}) collective-permute-start(bf16[2,2,128,128]{3,2,1,0:T(8,128)(2,1)S(1)} %slice.100), channel_id=1, source_target_pairs={{0,14},{2,0},{4,2},{6,4},{8,6},{10,8},{12,10},{14,12},{16,30},{18,... | collective-permute-start | bytes 393224 | tf_op jit(solution)/shard_map/ppermute | solution.py:300
  42.7 6.3 %collective-permute-start.8 = (bf16[2,2,128,128]{3,2,1,0:T(8,128)(2,1)S(1)}, bf16[2,2,128,128]{3,2,1,0:T(8,128)(2,1)S(1)}, u32[]{:S(2)}, u32[]{:S(2)}) collective-permute-start(bf16[2,2,128,128]{3,2,1,0:T(8,128)(2,1)S(1)} %slice.99), channel_id=1, source_target_pairs={{0,2},{2,4},{4,6},{6,8},{8,10},{10,12},{12,14},{14,0},{16,18},{18,... | collective-permute-start | bytes 393224 | tf_op jit(solution)/shard_map/ppermute | solution.py:296
  53.0 12.5 %collective-permute-start.14 = (bf16[2,2,128,128]{3,2,1,0:T(8,128)(2,1)S(1)}, bf16[2,2,128,128]{3,2,1,0:T(8,128)(2,1)S(1)}, u32[]{:S(2)}, u32[]{:S(2)}) collective-permute-start(bf16[2,2,128,128]{3,2,1,0:T(8,128)(2,1)S(1)} %get-tuple-element.49), channel_id=1, source_target_pairs={{0,2},{2,4},{4,6},{6,8},{8,10},{10,12},{12,14},{14,0},{16,18},{18,... | collective-permute-start | bytes 393224 | tf_op jit(solution)/shard_map/ppermute | solution.py:296
  53.5 12.2 %collective-permute-start.15 = (bf16[2,2,128,128]{3,2,1,0:T(8,128)(2,1)S(1)}, bf16[2,2,128,128]{3,2,1,0:T(8,128)(2,1)S(1)}, u32[]{:S(2)}, u32[]{:S(2)}) collective-permute-start(bf16[2,2,128,128]{3,2,1,0:T(8,128)(2,1)S(1)} %get-tuple-element.50), channel_id=1, source_target_pairs={{0,14},{2,0},{4,2},{6,4},{8,6},{10,8},{12,10},{14,12},{16,30},{18,... | collective-permute-start | bytes 393224 | tf_op jit(solution)/shard_map/ppermute | solution.py:300
  56.3 16.7 %collective-permute-start.13 = (bf16[1024,128]{1,0:T(8,128)(2,1)S(1)}, bf16[1024,128]{1,0:T(8,128)(2,1)S(1)}, u32[]{:S(2)}, u32[]{:S(2)}) collective-permute-start(bf16[1024,128]{1,0:T(8,128)(2,1)S(1)} %get-tuple-element.48), channel_id=1, source_target_pairs={{0,48},{2,50},{4,52},{6,54},{8,56},{10,58},{12,60},{14,62},{16,32}... | collective-permute-start | bytes 786440 | tf_op jit(solution)/shard_map/ppermute | solution.py:345
  65.6 9.5 %collective-permute-start.16 = (bf16[4,2,128,128]{3,2,1,0:T(8,128)(2,1)S(1)}, bf16[4,2,128,128]{3,2,1,0:T(8,128)(2,1)S(1)}, u32[]{:S(2)}, u32[]{:S(2)}) collective-permute-start(bf16[4,2,128,128]{3,2,1,0:T(8,128)(2,1)S(1)} %pad_maximum_fusion.3), channel_id=1, source_target_pairs={{0,2},{2,4},{4,6},{6,8},{8,10},{10,12},{12,14},{14,0},{16,18},{18,... | collective-permute-start | bytes 786440 | tf_op jit(solution)/shard_map/ppermute | solution.py:296
  65.8 9.5 %collective-permute-start.18 = (bf16[4,2,128,128]{3,2,1,0:T(8,128)(2,1)S(1)}, bf16[4,2,128,128]{3,2,1,0:T(8,128)(2,1)S(1)}, u32[]{:S(2)}, u32[]{:S(2)}) collective-permute-start(bf16[4,2,128,128]{3,2,1,0:T(8,128)(2,1)S(1)} %pad_maximum_fusion.4), channel_id=1, source_target_pairs={{0,14},{2,0},{4,2},{6,4},{8,6},{10,8},{12,10},{14,12},{16,30},{18,... | collective-permute-start | bytes 786440 | tf_op jit(solution)/shard_map/ppermute | solution.py:300
  75.2 8.7 %collective-permute-start.17 = (bf16[4,2,128,128]{3,2,1,0:T(8,128)(2,1)S(1)}, bf16[4,2,128,128]{3,2,1,0:T(8,128)(2,1)S(1)}, u32[]{:S(2)}, u32[]{:S(2)}) collective-permute-start(bf16[4,2,128,128]{3,2,1,0:T(8,128)(2,1)S(1)} %add_convert_fusion.3), channel_id=1, source_target_pairs={{0,2},{2,4},{4,6},{6,8},{8,10},{10,12},{12,14},{14,0},{16,18},{18,... | collective-permute-start | bytes 786440 | tf_op jit(solution)/shard_map/ppermute | solution.py:296
  75.4 8.6 %collective-permute-start.19 = (bf16[4,2,128,128]{3,2,1,0:T(8,128)(2,1)S(1)}, bf16[4,2,128,128]{3,2,1,0:T(8,128)(2,1)S(1)}, u32[]{:S(2)}, u32[]{:S(2)}) collective-permute-start(bf16[4,2,128,128]{3,2,1,0:T(8,128)(2,1)S(1)} %add_convert_fusion.2), channel_id=1, source_target_pairs={{0,14},{2,0},{4,2},{6,4},{8,6},{10,8},{12,10},{14,12},{16,30},{18,... | collective-permute-start | bytes 786440 | tf_op jit(solution)/shard_map/ppermute | solution.py:300
  83.9 8.4 %collective-permute-start.21 = (bf16[4,2,128,128]{3,2,1,0:T(8,128)(2,1)S(1)}, bf16[4,2,128,128]{3,2,1,0:T(8,128)(2,1)S(1)}, u32[]{:S(2)}, u32[]{:S(2)}) collective-permute-start(bf16[4,2,128,128]{3,2,1,0:T(8,128)(2,1)S(1)} %add_convert_fusion.1), channel_id=1, source_target_pairs={{0,2},{2,4},{4,6},{6,8},{8,10},{10,12},{12,14},{14,0},{16,18},{18,... | collective-permute-start | bytes 786440 | tf_op jit(solution)/shard_map/ppermute | solution.py:296
  84.1 8.2 %collective-permute-start.22 = (bf16[4,2,128,128]{3,2,1,0:T(8,128)(2,1)S(1)}, bf16[4,2,128,128]{3,2,1,0:T(8,128)(2,1)S(1)}, u32[]{:S(2)}, u32[]{:S(2)}) collective-permute-start(bf16[4,2,128,128]{3,2,1,0:T(8,128)(2,1)S(1)} %add_convert_fusion), channel_id=1, source_target_pairs={{0,14},{2,0},{4,2},{6,4},{8,6},{10,8},{12,10},{14,12},{16,30},{18,... | collective-permute-start | bytes 786440 | tf_op jit(solution)/shard_map/ppermute | solution.py:300
  91.3 7.7 %collective-permute-start.20 = (bf16[1024,128]{1,0:T(8,128)(2,1)S(1)}, bf16[1024,128]{1,0:T(8,128)(2,1)S(1)}, u32[]{:S(2)}, u32[]{:S(2)}) collective-permute-start(bf16[1024,128]{1,0:T(8,128)(2,1)S(1)} %get-tuple-element.62), channel_id=1, source_target_pairs={{0,48},{2,50},{4,52},{6,54},{8,56},{10,58},{12,60},{14,62},{16,32}... | collective-permute-start | bytes 786440 | tf_op jit(solution)/shard_map/ppermute | solution.py:361
  92.5 7.5 %collective-permute-start.23 = (bf16[2,128,128]{2,1,0:T(8,128)(2,1)S(1)}, bf16[2,128,128]{2,1,0:T(8,128)(2,1)S(1)}, u32[]{:S(2)}, u32[]{:S(2)}) collective-permute-start(bf16[2,128,128]{2,1,0:T(8,128)(2,1)S(1)} %get-tuple-element.88), channel_id=1, source_target_pairs={{0,48},{2,50},{4,52},{6,54},{8,56},{10,58},{12,60},{14,62},{16,0},... | collective-permute-start | bytes 196616 | tf_op jit(solution)/shard_map/ppermute | solution.py:371
  94.9 6.2 %collective-permute-start.25 = (bf16[2,128,128]{2,1,0:T(8,128)(2,1)S(1)}, bf16[2,128,128]{2,1,0:T(8,128)(2,1)S(1)}, u32[]{:S(2)}, u32[]{:S(2)}) collective-permute-start(bf16[2,128,128]{2,1,0:T(8,128)(2,1)S(1)} %get-tuple-element.89), channel_id=1, source_target_pairs={{0,16},{2,18},{4,20},{6,22},{8,24},{10,26},{12,28},{14,30},{16,32}... | collective-permute-start | bytes 196616 | tf_op jit(solution)/shard_map/ppermute | solution.py:371
  (7 other events, 21.8 us)

commit v2 on v1

v2 whole, which is shorter than its diff:
```python
import functools
import math

import jax
import jax.numpy as jnp
from jax import lax
from jax.experimental import pallas as pl
from jax.experimental.pallas import tpu as pltpu
from jax.sharding import PartitionSpec as P

MASKED_SCORE = -1e30
NY, NZ = 4, 8


def dot_tn(left, right):
    return lax.dot_general(left, right, (((0,), (0,)), ((), ())), preferred_element_type=jnp.float32)


def dot_nt(left, right):
    return lax.dot_general(left, right, (((1,), (1,)), ((), ())), preferred_element_type=jnp.float32)


def dot_nn(left, right):
    return jnp.dot(left, right, preferred_element_type=jnp.float32)


def stage_kernel(stage, waits, passing, block, group, *refs):
    offset, forward, finish, backward, last = stage
    first = forward and offset == 0
    paired = offset not in (0, 4)
    units = 4 if paired else 2
    lanes = block * group
    refs = list(refs)
    take = lambda count: [refs.pop(0) for _ in range(count)]
    take(waits)
    docs_ref, place_ref = take(2)
    q_in = take(2)
    g_in = take(2) if backward else []
    pieces = take(1 if offset == 0 else 2)
    state_in = take(3) if forward and not first else []
    stats_in = take(2) if backward and not finish else []
    dq_in = take(1) if backward and not finish else []
    take(passing)
    state_out = take(3) if forward and not finish else []
    rows_out = take(2) if finish or last else []
    stats_out = take(2) if finish else []
    dq_out = take(1) if backward and not last else []
    grads = take(len(pieces)) if backward else []
    take(passing)
    k_scr, v_scr, q_scr, s_scr, m_scr = take(5)
    if finish:
        state_out = take(3)
    if backward:
        g_scr, dk_scr, dv_scr = take(3)
    if last:
        dq_out = take(1)
    stats = stats_out or stats_in

    head_size = q_in[0].shape[1]
    scale = 1.0 / math.sqrt(head_size)
    log2_scale = scale * math.log2(math.e)
    y, z = place_ref[0], place_ref[1]

    def block_of(slot, distance):
        return (y ^ slot) * NZ + lax.rem(z + NZ + distance, NZ)

    def blocks_of(unit):
        if paired:
            ahead = jnp.where(lax.rem(z, 2) == 0, offset, -offset)
            return block_of(unit, ahead), block_of(unit, -ahead)
        return block_of(2 * unit, offset), block_of(2 * unit + 1, offset)

    def places():
        for unit in range(units):
            for half in range(2):
                if paired:
                    yield unit, half, half, unit
                else:
                    yield unit, half, unit if offset else 0, half if offset else 2 * unit + half

    for unit, half, piece, slot in places():
        rows = pl.ds(half * block, block)
        k_scr[unit, rows, :] = pieces[piece][slot, 0]
        v_scr[unit, rows, :] = pieces[piece][slot, 1]
    for part in range(2):
        q_scr[part] = q_in[part][...]
        if backward:
            g_scr[part] = g_in[part][...]

    def doc_start(position):
        bound, start = jnp.int32(0), jnp.zeros_like(position)
        for number in range(docs_ref.shape[0]):
            bound = bound + docs_ref[number]
            start = jnp.where(bound <= position, bound, start)
        return start

    def fold(value):
        return value.reshape(value.shape[0] // 8, 8, value.shape[1])

    def part_facts(part):
        query_block = jnp.where(part == 0, y, NY - 1 - y) * NZ + z
        first_pos = query_block * block
        return query_block, doc_start(first_pos), doc_start(first_pos + block - 1)

    def is_live(unit, facts):
        query_block, open_first, _ = facts
        return [(n <= query_block) & ((n + 1) * block > open_first) for n in blocks_of(unit)]

    def is_clear(unit, facts):
        query_block, _, open_last = facts
        one, two = ((n < query_block) & (n * block >= open_last) for n in blocks_of(unit))
        return one & two

    def scores_of(unit, rows, part, facts, masked):
        scores = dot_nt(k_scr[unit, rows, :], q_scr[part])
        if masked:
            lane = lax.broadcasted_iota(jnp.int32, (1, lanes), 1)
            positions = facts[0] * block + lane // group
            one, two = blocks_of(unit)
            row = lax.broadcasted_iota(jnp.int32, scores.shape, 0)
            if scores.shape[0] == block:
                key_pos = row + jnp.where(rows.start == 0, one, two) * block
            else:
                key_pos = row + jnp.where(row < block, one, two - 1) * block
            allowed = (key_pos <= positions) & (key_pos >= doc_start(positions))
            scores = jnp.where(allowed, scores, MASKED_SCORE)
        return scores

    def each_unit(facts, work, masks=True):
        def step(unit, _):
            one, two = is_live(unit, facts)
            both, whole = one & two, pl.ds(0, 2 * block)
            if masks:
                clear = is_clear(unit, facts)
                pl.when(both & clear)(lambda: work(unit, whole, False))
                pl.when(both & jnp.logical_not(clear))(lambda: work(unit, whole, True))
            else:
                pl.when(both)(lambda: work(unit, whole, False))
            half = pl.ds(pl.multiple_of(jnp.where(one, 0, block), block), block)
            pl.when(one ^ two)(lambda: work(unit, half, masks))
            return 0

        lax.fori_loop(0, units, step, 0)

    def forward_part(part, _):
        facts = part_facts(part)
        m_new, l_new, o_new = state_out
        if first:
            m_old = jnp.full((8, lanes), MASKED_SCORE, jnp.float32)
        else:
            m_old = state_in[0][part]
        m_scr[...] = m_old

        def score(unit, rows, masked):
            scores = scores_of(unit, rows, part, facts, masked)
            s_scr[unit, rows, :] = scores
            m_scr[...] = jnp.maximum(m_scr[...], jnp.max(fold(scores), axis=0))

        each_unit(facts, score)
        top = jnp.max(m_scr[...], axis=0, keepdims=True)
        m_new[part] = jnp.broadcast_to(top, (8, lanes))
        if first:
            l_new[part] = jnp.zeros((8, lanes), jnp.float32)
            o_new[part] = jnp.zeros((head_size, lanes), jnp.float32)
        else:
            fading = jnp.exp2((m_old - top) * log2_scale)
            l_new[part] = state_in[1][part] * fading
            o_new[part] = state_in[2][part] * fading[:1]
        row_max = top * log2_scale

        def weigh(unit, rows, _):
            weights = jnp.exp2(s_scr[unit, rows, :] * log2_scale - row_max)
            l_new[part] += jnp.sum(fold(weights), axis=0)
            o_new[part] += dot_tn(v_scr[unit, rows, :], weights.astype(jnp.bfloat16))

        each_unit(facts, weigh, masks=False)
        if finish:
            row_total = jnp.sum(l_new[part], axis=0, keepdims=True)
            attended = (o_new[part] / row_total).T.astype(jnp.bfloat16)
            products = attended.astype(jnp.float32) * g_scr[part].astype(jnp.float32)
            stats_out[0][part] = jnp.broadcast_to(row_max + jnp.log2(row_total), (8, lanes))
            upper = products.astype(jnp.bfloat16)
            lower = (products - upper.astype(jnp.float32)).astype(jnp.bfloat16)
            ones = jnp.ones((8, head_size), jnp.bfloat16)
            stats_out[1][part] = dot_nt(ones, upper) + dot_nt(ones, lower)
            write_rows(part, attended)
        return 0

    def write_rows(part, rows):
        for number in range(2):

            @pl.when(part == number)
            def _():
                rows_out[number][...] = rows

    def backward_part(part, _):
        facts = part_facts(part)
        log_total, out_dot = stats[0][part][:1], stats[1][part][:1]
        dq_new = dq_out[0]
        dq_new[part] = jnp.zeros((head_size, lanes), jnp.float32) if finish else dq_in[0][part]

        def differentiate(unit, rows, masked):
            probs = jnp.exp2(scores_of(unit, rows, part, facts, masked) * log2_scale - log_total)
            dprobs = dot_nt(v_scr[unit, rows, :], g_scr[part])
            dscores = (probs * (dprobs - out_dot)).astype(jnp.bfloat16)
            dv_scr[unit, rows, :] += dot_nn(probs.astype(jnp.bfloat16), g_scr[part])
            dk_scr[unit, rows, :] += dot_nn(dscores, q_scr[part])
            dq_new[part] += dot_tn(k_scr[unit, rows, :], dscores)

        each_unit(facts, differentiate)
        if last:
            write_rows(part, (dq_new[part] * scale).T.astype(jnp.bfloat16))
        return 0

    if forward:
        lax.fori_loop(0, 2, forward_part, 0)
    if backward:
        dk_scr[...] = jnp.zeros_like(dk_scr)
        dv_scr[...] = jnp.zeros_like(dv_scr)
        lax.fori_loop(0, 2, backward_part, 0)
        for unit, half, piece, slot in places():
            rows = pl.ds(half * block, block)
            grads[piece][slot, 0] = (dk_scr[unit, rows, :] * scale).astype(jnp.bfloat16)
            grads[piece][slot, 1] = dv_scr[unit, rows, :].astype(jnp.bfloat16)


def run_stage(stage, block, group, facts, q_parts, g_parts, pieces, state=(), stats=(), dq=(), after=(), passing=()):
    offset, forward, finish, backward, last = stage
    units = 2 if offset in (0, 4) else 4
    lanes, head_size = q_parts[0].shape
    f32 = lambda *shape: jax.ShapeDtypeStruct(shape, jnp.float32)
    low = lambda array: jax.ShapeDtypeStruct(array.shape, jnp.bfloat16)
    state_shapes = [f32(2, 8, lanes), f32(2, 8, lanes), f32(2, head_size, lanes)]
    dq_shape = f32(2, head_size, lanes)
    operands = [*after, *facts, *q_parts, *(g_parts if backward else ()), *pieces, *state, *stats, *dq, *passing]
    outs = []
    aliases = {}
    if forward and not finish:
        if state:
            aliases = {len(operands) - 3 + n: n for n in range(3)}
        outs += state_shapes
    if finish or last:
        outs += [low(q) for q in q_parts]
    if finish:
        outs += state_shapes[:2]
    if backward and not last:
        if dq:
            aliases = {len(operands) - 1: len(outs)}
        outs += [dq_shape]
    if backward:
        outs += [low(piece) for piece in pieces]
    for number, array in enumerate(passing):
        aliases[len(operands) - len(passing) + number] = len(outs)
        outs += [low(array)]
    scratch = [
        pltpu.VMEM((units, 2 * block, head_size), jnp.bfloat16),
        pltpu.VMEM((units, 2 * block, head_size), jnp.bfloat16),
        pltpu.VMEM((2, lanes, head_size), jnp.bfloat16),
        pltpu.VMEM((units if forward else 1, 2 * block, lanes), jnp.float32),
        pltpu.VMEM((8, lanes), jnp.float32),
    ]
    if finish:
        scratch += [pltpu.VMEM(shape.shape, jnp.float32) for shape in state_shapes]
    if backward:
        scratch += [
            pltpu.VMEM((2, lanes, head_size), jnp.bfloat16),
            pltpu.VMEM((units, 2 * block, head_size), jnp.float32),
            pltpu.VMEM((units, 2 * block, head_size), jnp.float32),
        ]
    if last:
        scratch += [pltpu.VMEM(dq_shape.shape, jnp.float32)]
    smem = pl.BlockSpec(memory_space=pltpu.SMEM)
    vmem = pl.BlockSpec(memory_space=pltpu.VMEM)
    anywhere = pl.BlockSpec(memory_space=pl.ANY)
    inside = len(operands) - 2 - len(after) - len(passing)
    products = 2 * forward + 5 * backward
    return pl.pallas_call(
        functools.partial(stage_kernel, stage, len(after), len(passing), block, group),
        out_shape=outs,
        in_specs=[anywhere] * len(after) + [smem, smem] + [vmem] * inside + [anywhere] * len(passing),
        out_specs=[vmem] * (len(outs) - len(passing)) + [anywhere] * len(passing),
        scratch_shapes=scratch,
        input_output_aliases=aliases,
        compiler_params=pltpu.CompilerParams(vmem_limit_bytes=24 * 1024 * 1024),
        cost_estimate=pl.CostEstimate(
            flops=6 * products * 2 * lanes * units * 2 * block * head_size,
            bytes_accessed=4 * 1024 * 1024,
            transcendentals=2 * lanes * units * 2 * block,
        ),
        name="fwd" * forward + "bwd" * backward + str(offset),
    )(*operands)


def swap_y(mask):
    return [(y * NZ + z, (y ^ mask) * NZ + z) for y in range(NY) for z in range(NZ)]


def swap_z(first):
    turns = [1 if z % 2 == first else -1 for z in range(NZ)]
    return [(y * NZ + z, y * NZ + (z + turns[z]) % NZ) for y in range(NY) for z in range(NZ)]


MIRROR = swap_y(NY - 1)


def add_up(one, other):
    return (one.astype(jnp.float32) + other.astype(jnp.float32)).astype(jnp.bfloat16)


def swap_even(array):
    return lax.ppermute(array, "ctx", swap_z(0))


def swap_odd(array):
    return lax.ppermute(array, "ctx", swap_z(1))


def on_device(queries, key_rows, values, out_grad, doc_lengths):
    block, query_heads, head_size = queries.shape
    key_heads = key_rows.shape[1]
    group = query_heads // key_heads
    place = lax.axis_index("ctx")
    y, z = place // NZ, place % NZ
    mine = y // 2

    def head_of(array, number, width):
        picked = jnp.where(number == 0, array[:, :width], array[:, width:])
        return picked.reshape(block * width, head_size)

    def key_pair(number):
        return jnp.stack([head_of(key_rows, number, 1), head_of(values, number, 1)])

    pairs = [key_pair(mine), key_pair(1 - mine)]
    held = {mask: lax.ppermute(pairs[mask // 2], "ctx", swap_y(mask)) for mask in (1, 3, 2)}
    column = jnp.stack([pairs[0], held[1], held[2], held[3]])

    q_parts = [head_of(queries, mine, group), lax.ppermute(head_of(queries, 1 - mine, group), "ctx", MIRROR)]
    g_own, g_leaving = head_of(out_grad, mine, group), head_of(out_grad, 1 - mine, group)
    facts = (doc_lengths, jnp.stack([y, z]).astype(jnp.int32))
    run = functools.partial(run_stage, block=block, group=group, facts=facts, q_parts=q_parts)

    evens, odds = [column], [column]
    state = ()
    for step in range(4):
        pieces = [column] if step == 0 else [evens[step], odds[step]]
        if step < 3:
            even, odd = swap_even(odds[step]), swap_odd(evens[step])
        else:
            even, odd = swap_even(odds[step][:2]), swap_odd(evens[step][2:])
        evens.append(even)
        odds.append(odd)
        passing = () if step else (g_leaving,)
        state = run((step, True, False, False, False), g_parts=(), pieces=pieces, state=state, passing=passing)
        if passing:
            g_parts = [g_own, lax.ppermute(state[3], "ctx", MIRROR)]
            state = state[:3]
    run = functools.partial(run, g_parts=g_parts)
    own_out, other_out, log_total, out_dot, dq, even_grad, odd_grad = run(
        (4, True, True, True, False), pieces=[evens[4], odds[4]], state=state
    )
    stats = (log_total, out_dot)
    other_out = lax.ppermute(other_out, "ctx", MIRROR)
    even, odd = swap_even(even_grad), swap_odd(odd_grad)
    after = ()
    for step in (3, 2, 1):
        dq, even_grad, odd_grad = run(
            (step, False, False, True, False), pieces=[evens[step], odds[step]], stats=stats, dq=(dq,), after=after
        )
        if step == 3:
            odd_grad = jnp.concatenate([add_up(odd_grad[:2], even), odd_grad[2:]], axis=0)
            even_grad = jnp.concatenate([even_grad[:2], add_up(even_grad[2:], odd)], axis=0)
        else:
            odd_grad, even_grad = add_up(odd_grad, even), add_up(even_grad, odd)
        after = (even, odd)
        even, odd = swap_even(even_grad), swap_odd(odd_grad)
    own_dq, other_dq, grad = run((0, False, False, True, True), pieces=[column], stats=stats, dq=(dq,), after=after)
    other_dq = lax.ppermute(other_dq, "ctx", MIRROR)
    sums = grad.astype(jnp.float32) + even.astype(jnp.float32) + odd.astype(jnp.float32)

    def both_heads(own, other):
        one, two = (r.reshape(block, group, head_size) for r in (own, other))
        return jnp.concatenate([jnp.where(mine == 0, one, two), jnp.where(mine == 0, two, one)], axis=1)

    attended, query_grad = both_heads(own_out, other_out), both_heads(own_dq, other_dq)
    arrived = {
        mask: lax.ppermute(sums[mask].astype(jnp.bfloat16), "ctx", swap_y(mask)).astype(jnp.float32)
        for mask in (1, 3, 2)
    }
    near, far = sums[0] + arrived[1], arrived[2] + arrived[3]
    heads = [jnp.where(mine == 0, near, far), jnp.where(mine == 0, far, near)]
    grads = jnp.stack(heads, axis=2).astype(jnp.bfloat16)
    return attended, query_grad, grads[0], grads[1]


def solution(mesh):
    placed = (
        P(("dp", "ctx"), "head", None),
        P(("dp", "ctx"), "head", None),
        P(("dp", "ctx"), "head", None),
        P(("dp", "ctx"), "head", None),
        P("dp"),
    )
    return jax.shard_map(
        on_device,
        mesh=mesh,
        in_specs=placed,
        out_specs=(
            P(("dp", "ctx"), "head", None),
            P(("dp", "ctx"), "head", None),
            P(("dp", "ctx"), "head", None),
            P(("dp", "ctx"), "head", None),
        ),
        check_vma=False,
    )
```

time: 104 us -> 97.9 us (0.941)
  starting transfers between devices: 49.9 us -> 29.8 us
  waiting for transfers between devices: 13.2 us -> 25.5 us
  Pallas kernels: 31.7 us -> 34.3 us
    ppermute x24, starting transfers between devices: 43.5 us -> 27 us  [the longest x8 11 us: swap_odd(): return lax.ppermute(array, 'ctx', swap_z(1))]
    ppermute x24, waiting for transfers between devices: 10.6 us -> 25.4 us  [the longest x8 11.4 us: swap_even(): return lax.ppermute(array, 'ctx', swap_z(0))]
    ppermute x1, starting transfers between devices: 5.44 us -> 0.25 us  [on_device(): other_out = lax.ppermute(other_out, 'ctx', MIRROR)]
    pallas_call x9, Pallas kernels: 31.7 us -> 34.3 us  [run_stage(): pl.pallas_call(functools.partial(stage_kernel, stage, len(after), len(pas...]
    ppermute x1, waiting for transfers between devices: 2.57 us -> 0.08 us  [on_device(): other_dq = lax.ppermute(other_dq, 'ctx', MIRROR)]
    ppermute x1, starting transfers between devices: 0.96 us -> 2.52 us  [on_device(): other_dq = lax.ppermute(other_dq, 'ctx', MIRROR)]
  transfers between devices with their start and end apart: 26 -> 26, of which waited for: 10 -> 14; matrix products, arithmetic and copies ran while one was open for 3% -> 3% of each run, Pallas kernels for 27% -> 30%
where the time goes in v2:
time: 97.9 us; the launch traced here: 97.1 us
  Pallas kernels  34.3 us (35%)
  starting transfers between devices  29.8 us (30%)
  waiting for transfers between devices  25.5 us (26%)
  local copies, waits for them, and re-layouts  3.84 us (4%)
  other arithmetic  2.66 us (3%)
  between operations  1.04 us (1%)
    pallas_call x9, Pallas kernels, run_stage(): pl.pallas_call(functools.partial(stage_kernel, stage, len(after), len(pas...  34.3 us
    ppermute x8, waiting for transfers between devices, swap_even(): return lax.ppermute(array, 'ctx', swap_z(0))  11.4 us
    ppermute x8, starting transfers between devices, swap_odd(): return lax.ppermute(array, 'ctx', swap_z(1))  11 us
    ppermute x8, waiting for transfers between devices, swap_odd(): return lax.ppermute(array, 'ctx', swap_z(1))  10 us
    ppermute x3, starting transfers between devices, on_device(): lax.ppermute(pairs[mask // 2], 'ctx', swap_y(mask))  4.27 us
    ppermute x3, starting transfers between devices, on_device(): lax.ppermute(sums[mask].astype(jnp.bfloat16), 'ctx', swap_y(mask))  4.18 us
    unnamed x12, local copies, waits for them, and re-layouts  3.59 us
    ppermute x1, starting transfers between devices, on_device(): lax.ppermute(head_of(queries, 1 - mine, group), 'ctx', MIRROR)  3.1 us
  transfers between devices with their start and end apart: 26, of which 14 were waited for; matrix products, arithmetic and copies ran while one was open for 3% of the time, Pallas kernels for 30%

profile of v2, /device:TPU:6, one launch (start us, length us, event | category | flops | bytes accessed | tf_op | source)
XLA Modules:
  0.0 97.1 jit_solution(13487072321228883892)
XLA Ops:
  2.5 3.1 %collective-permute-start.3 = (bf16[2,128,128]{2,1,0:T(8,128)(2,1)S(1)}, bf16[2,128,128]{2,1,0:T(8,128)(2,1)S(1)}, u32[]{:S(2)}, u32[]{:S(2)}) collective-permute-start(bf16[2,128,128]{2,1,0:T(8,128)(2,1)S(1)} %pad_maximum_fusion.7), channel_id=1, source_target_pairs={{0,48},{2,50},{4,52},{6,54},{8,56},{10,58},{12,60},{14,62},{16,32}... | collective-permute-start | bytes 196616 | tf_op jit(solution)/shard_map/ppermute | solution.py:334
  6.8 3.1 %collective-permute-start = (bf16[1024,128]{1,0:T(8,128)(2,1)S(1)}, bf16[1024,128]{1,0:T(8,128)(2,1)S(1)}, u32[]{:S(2)}, u32[]{:S(2)}) collective-permute-start(bf16[1024,128]{1,0:T(8,128)(2,1)S(1)} %get-tuple-element.82), channel_id=1, source_target_pairs={{0,48},{2,50},{4,52},{6,54},{8,56},{10,58},{12,60},{14,62},{16,32}... | collective-permute-start | bytes 786440 | tf_op jit(solution)/shard_map/ppermute | solution.py:337
  11.4 2.0 %collective-permute-start.9 = (bf16[4,2,128,128]{3,2,1,0:T(8,128)(2,1)S(1)}, bf16[4,2,128,128]{3,2,1,0:T(8,128)(2,1)S(1)}, u32[]{:S(2)}, u32[]{:S(2)}) collective-permute-start(bf16[4,2,128,128]{3,2,1,0:T(8,128)(2,1)S(1)} %pad_maximum_fusion.2.refs_4_.refs_8_), channel_id=1, source_target_pairs={{0,2},{2,0},{4,6},{6,4},{8,10},{10,8},{12,14},{14,12},{16,18},{18,... | collective-permute-start | bytes 786440 | tf_op jit(solution)/shard_map/ppermute | solution.py:311
  13.4 4.9 %collective-permute-start.5 = (bf16[4,2,128,128]{3,2,1,0:T(8,128)(2,1)S(1)}, bf16[4,2,128,128]{3,2,1,0:T(8,128)(2,1)S(1)}, u32[]{:S(2)}, u32[]{:S(2)}) collective-permute-start(bf16[4,2,128,128]{3,2,1,0:T(8,128)(2,1)S(1)} %pad_maximum_fusion.2.refs_4_.refs_8_), channel_id=1, source_target_pairs={{0,14},{2,4},{4,2},{6,8},{8,6},{10,12},{12,10},{14,0},{16,30},{18,... | collective-permute-start | bytes 786440 | tf_op jit(solution)/shard_map/ppermute | solution.py:315
  19.1 2.8 %fwd0.1 = (f32[2,8,1024]{2,1,0:T(8,128)S(1)}, f32[2,8,1024]{2,1,0:T(8,128)S(1)}, f32[2,128,1024]{2,1,0:T(8,128)S(1)}, bf16[1024,128]{1,0:T(8,128)(2,1)S(1)}) custom-call(s32[16]{0:T(128)S(1)} %copy-done, s32[2]{0:T(128)S(1)} %pad_add_fusion.refs_1_.refs_3_, bf16[1024,128]{1,0:T(8,128)(2,1)S(1)} %get-tuple-element.83.refs_2_.refs_4_, ...), custom_call_target="tpu_custom_call", output_to_operand_aliasing={{3}: (5, {})} | custom-call | flops 1610612736 | bytes 4194304 | tf_op jit(solution)/shard_map/fwd0/pallas_call | solution.py:277
  23.4 3.5 %collective-permute-start.10 = (bf16[4,2,128,128]{3,2,1,0:T(8,128)(2,1)S(1)}, bf16[4,2,128,128]{3,2,1,0:T(8,128)(2,1)S(1)}, u32[]{:S(2)}, u32[]{:S(2)}) collective-permute-start(bf16[4,2,128,128]{3,2,1,0:T(8,128)(2,1)S(1)} %collective-permute-done.9.refs_4_.refs_8_), channel_id=1, source_target_pairs={{0,14},{2,4},{4,2},{6,8},{8,6},{10,12},{12,10},{14,0},{16,30},{18,... | collective-permute-start | bytes 786440 | tf_op jit(solution)/shard_map/ppermute | solution.py:315
  26.9 3.4 %fwd1.1 = (f32[2,8,1024]{2,1,0:T(8,128)S(1)}, f32[2,8,1024]{2,1,0:T(8,128)S(1)}, f32[2,128,1024]{2,1,0:T(8,128)S(1)}) custom-call(s32[16]{0:T(128)S(1)} %copy-done, s32[2]{0:T(128)S(1)} %pad_add_fusion.refs_1_.refs_3_, bf16[1024,128]{1,0:T(8,128)(2,1)S(1)} %get-tuple-element.83.refs_2_.refs_4_, ...), custom_call_target="tpu_custom_call", output_to_operand_aliasing={{0}: (6, {}), {1}: (7, {}), {2}: (8, {})} | custom-call | flops 3221225472 | bytes 4194304 | tf_op jit(solution)/shard_map/fwd1/pallas_call | solution.py:277
  31.3 4.2 %collective-permute-done.6.refs_4_.refs_8_ = bf16[4,2,128,128]{3,2,1,0:T(8,128)(2,1)S(1)} collective-permute-done((bf16[4,2,128,128]{3,2,1,0:T(8,128)(2,1)S(1)}, bf16[4,2,128,128]{3,2,1,0:T(8,128)(2,1)S(1)}, u32[]{:S(2)}, u32[]{:S(2)}) %collective-permute-start.6) | collective-permute-done | bytes 262176 | tf_op jit(solution)/shard_map/ppermute | solution.py:311
  35.5 3.4 %fwd2.1 = (f32[2,8,1024]{2,1,0:T(8,128)S(1)}, f32[2,8,1024]{2,1,0:T(8,128)S(1)}, f32[2,128,1024]{2,1,0:T(8,128)S(1)}) custom-call(s32[16]{0:T(128)S(1)} %copy-done, s32[2]{0:T(128)S(1)} %pad_add_fusion.refs_1_.refs_3_, bf16[1024,128]{1,0:T(8,128)(2,1)S(1)} %get-tuple-element.83.refs_2_.refs_4_, ...), custom_call_target="tpu_custom_call", output_to_operand_aliasing={{0}: (6, {}), {1}: (7, {}), {2}: (8, {})} | custom-call | flops 3221225472 | bytes 4194304 | tf_op jit(solution)/shard_map/fwd2/pallas_call | solution.py:277
  39.0 1.9 %collective-permute-start.12 = (bf16[2,2,128,128]{3,2,1,0:T(8,128)(2,1)S(1)}, bf16[2,2,128,128]{3,2,1,0:T(8,128)(2,1)S(1)}, u32[]{:S(2)}, u32[]{:S(2)}) collective-permute-start(bf16[2,2,128,128]{3,2,1,0:T(8,128)(2,1)S(1)} %slice.92), channel_id=1, source_target_pairs={{0,14},{2,4},{4,2},{6,8},{8,6},{10,12},{12,10},{14,0},{16,30},{18,... | collective-permute-start | bytes 393224 | tf_op jit(solution)/shard_map/ppermute | solution.py:315
  40.9 3.6 %collective-permute-done.7.refs_5_.refs_7_ = bf16[4,2,128,128]{3,2,1,0:T(8,128)(2,1)S(1)} collective-permute-done((bf16[4,2,128,128]{3,2,1,0:T(8,128)(2,1)S(1)}, bf16[4,2,128,128]{3,2,1,0:T(8,128)(2,1)S(1)}, u32[]{:S(2)}, u32[]{:S(2)}) %collective-permute-start.7) | collective-permute-done | bytes 262176 | tf_op jit(solution)/shard_map/ppermute | solution.py:315
  44.8 3.4 %fwd3.1 = (f32[2,8,1024]{2,1,0:T(8,128)S(1)}, f32[2,8,1024]{2,1,0:T(8,128)S(1)}, f32[2,128,1024]{2,1,0:T(8,128)S(1)}) custom-call(s32[16]{0:T(128)S(1)} %copy-done, s32[2]{0:T(128)S(1)} %pad_add_fusion.refs_1_.refs_3_, bf16[1024,128]{1,0:T(8,128)(2,1)S(1)} %get-tuple-element.83.refs_2_.refs_4_, ...), custom_call_target="tpu_custom_call", output_to_operand_aliasing={{0}: (6, {}), {1}: (7, {}), {2}: (8, {})} | custom-call | flops 3221225472 | bytes 4194304 | tf_op jit(solution)/shard_map/fwd3/pallas_call | solution.py:277
  49.7 4.8 %fwdbwd4.1 = (bf16[1024,128]{1,0:T(8,128)(2,1)S(1)}, bf16[1024,128]{1,0:T(8,128)(2,1)S(1)}, f32[2,8,1024]{2,1,0:T(8,128)S(1)}, f32[2,8,1024]{2,1,0:T(8,128)S(1)}...) custom-call(s32[16]{0:T(128)S(1)} %copy-done, ...), custom_call_target="tpu_custom_call" | custom-call | flops 5637144576 | bytes 4194304 | tf_op jit(solution)/shard_map/fwdbwd4/pallas_call | solution.py:277
  55.0 4.2 %bwd3.1 = (f32[2,128,1024]{2,1,0:T(8,128)S(1)}, bf16[4,2,128,128]{3,2,1,0:T(8,128)(2,1)S(1)}, bf16[4,2,128,128]{3,2,1,0:T(8,128)(2,1)S(1)}) custom-call(s32[16]{0:T(128)S(1)} %copy-done, s32[2]{0:T(128)S(1)} %pad_add_fusion.refs_1_.refs_3_, bf16[1024,128]{1,0:T(8,128)(2,1)S(1)} %get-tuple-element.83.refs_2_.refs_4_, ...), custom_call_target="tpu_custom_call", output_to_operand_aliasing={{0}: (10, {})} | custom-call | flops 8053063680 | bytes 4194304 | tf_op jit(solution)/shard_map/bwd3/pallas_call | solution.py:277
  59.3 1.7 %collective-permute-done.14.refs_0_ = bf16[2,2,128,128]{3,2,1,0:T(8,128)(2,1)S(1)} collective-permute-done((bf16[2,2,128,128]{3,2,1,0:T(8,128)(2,1)S(1)}, bf16[2,2,128,128]{3,2,1,0:T(8,128)(2,1)S(1)}, u32[]{:S(2)}, u32[]{:S(2)}) %collective-permute-start.14) | collective-permute-done | bytes 131104 | tf_op jit(solution)/shard_map/ppermute | solution.py:311
  62.5 4.2 %bwd2.1 = (f32[2,128,1024]{2,1,0:T(8,128)S(1)}, bf16[4,2,128,128]{3,2,1,0:T(8,128)(2,1)S(1)}, bf16[4,2,128,128]{3,2,1,0:T(8,128)(2,1)S(1)}) custom-call(bf16[2,2,128,128]{3,2,1,0:T(8,128)(2,1)S(1)} %collective-permute-done.14.refs_0_, bf16[2,2,128,128]{3,2,1,0:T(8,128)(2,1)S(1)} %collective-permute-done.15.refs_1_, ...), custom_call_target="tpu_custom_call", output_to_operand_aliasing={{0}: (12, {})} | custom-call | flops 8053063680 | bytes 4194304 | tf_op jit(solution)/shard_map/bwd2/pallas_call | solution.py:277
  67.6 3.9 %collective-permute-done.16.refs_1_ = bf16[4,2,128,128]{3,2,1,0:T(8,128)(2,1)S(1)} collective-permute-done((bf16[4,2,128,128]{3,2,1,0:T(8,128)(2,1)S(1)}, bf16[4,2,128,128]{3,2,1,0:T(8,128)(2,1)S(1)}, u32[]{:S(2)}, u32[]{:S(2)}) %collective-permute-start.16) | collective-permute-done | bytes 262176 | tf_op jit(solution)/shard_map/ppermute | solution.py:315
  71.9 4.2 %bwd1.1 = (f32[2,128,1024]{2,1,0:T(8,128)S(1)}, bf16[4,2,128,128]{3,2,1,0:T(8,128)(2,1)S(1)}, bf16[4,2,128,128]{3,2,1,0:T(8,128)(2,1)S(1)}) custom-call(bf16[4,2,128,128]{3,2,1,0:T(8,128)(2,1)S(1)} %collective-permute-done.18.refs_0_, bf16[4,2,128,128]{3,2,1,0:T(8,128)(2,1)S(1)} %collective-permute-done.16.refs_1_, ...), custom_call_target="tpu_custom_call", output_to_operand_aliasing={{0}: (12, {})} | custom-call | flops 8053063680 | bytes 4194304 | tf_op jit(solution)/shard_map/bwd1/pallas_call | solution.py:277
  76.1 3.9 %collective-permute-done.17.refs_0_ = bf16[4,2,128,128]{3,2,1,0:T(8,128)(2,1)S(1)} collective-permute-done((bf16[4,2,128,128]{3,2,1,0:T(8,128)(2,1)S(1)}, bf16[4,2,128,128]{3,2,1,0:T(8,128)(2,1)S(1)}, u32[]{:S(2)}, u32[]{:S(2)}) %collective-permute-start.17) | collective-permute-done | bytes 262176 | tf_op jit(solution)/shard_map/ppermute | solution.py:311
  80.7 3.8 %bwd0.1 = (bf16[1024,128]{1,0:T(8,128)(2,1)S(1)}, bf16[1024,128]{1,0:T(8,128)(2,1)S(1)}, bf16[4,2,128,128]{3,2,1,0:T(8,128)(2,1)S(1)}) custom-call(bf16[4,2,128,128]{3,2,1,0:T(8,128)(2,1)S(1)} %collective-permute-done.17.refs_0_, bf16[4,2,128,128]{3,2,1,0:T(8,128)(2,1)S(1)} %collective-permute-done.19.refs_1_, s32[16]{0:T(128)S(1)} %copy-done, ...), custom_call_target="tpu_custom_call" | custom-call | flops 4026531840 | bytes 4194304 | tf_op jit(solution)/shard_map/bwd0/pallas_call | solution.py:277
  84.5 2.5 %collective-permute-start.20 = (bf16[1024,128]{1,0:T(8,128)(2,1)S(1)}, bf16[1024,128]{1,0:T(8,128)(2,1)S(1)}, u32[]{:S(2)}, u32[]{:S(2)}) collective-permute-start(bf16[1024,128]{1,0:T(8,128)(2,1)S(1)} %get-tuple-element.64), channel_id=1, source_target_pairs={{0,48},{2,50},{4,52},{6,54},{8,56},{10,58},{12,60},{14,62},{16,32}... | collective-permute-start | bytes 786440 | tf_op jit(solution)/shard_map/ppermute | solution.py:377
  88.0 1.9 %collective-permute-start.25 = (bf16[2,128,128]{2,1,0:T(8,128)(2,1)S(1)}, bf16[2,128,128]{2,1,0:T(8,128)(2,1)S(1)}, u32[]{:S(2)}, u32[]{:S(2)}) collective-permute-start(bf16[2,128,128]{2,1,0:T(8,128)(2,1)S(1)} %get-tuple-element.85), channel_id=1, source_target_pairs={{0,48},{2,50},{4,52},{6,54},{8,56},{10,58},{12,60},{14,62},{16,32}... | collective-permute-start | bytes 196616 | tf_op jit(solution)/shard_map/ppermute | solution.py:386
  89.9 2.2 %collective-permute-start.24 = (bf16[2,128,128]{2,1,0:T(8,128)(2,1)S(1)}, bf16[2,128,128]{2,1,0:T(8,128)(2,1)S(1)}, u32[]{:S(2)}, u32[]{:S(2)}) collective-permute-start(bf16[2,128,128]{2,1,0:T(8,128)(2,1)S(1)} %get-tuple-element.86), channel_id=1, source_target_pairs={{0,32},{2,34},{4,36},{6,38},{8,40},{10,42},{12,44},{14,46},{16,48}... | collective-permute-start | bytes 196616 | tf_op jit(solution)/shard_map/ppermute | solution.py:386
  93.6 2.1 %collective-permute-done.24 = bf16[2,128,128]{2,1,0:T(8,128)(2,1)S(1)} collective-permute-done((bf16[2,128,128]{2,1,0:T(8,128)(2,1)S(1)}, bf16[2,128,128]{2,1,0:T(8,128)(2,1)S(1)}, u32[]{:S(2)}, u32[]{:S(2)}) %collective-permute-start.24) | collective-permute-done | bytes 65568 | tf_op jit(solution)/shard_map/ppermute | solution.py:386
  (78 shorter events, 17.2 us)
Async XLA Ops:
  2.5 8.1 %collective-permute-start.3 = (bf16[2,128,128]{2,1,0:T(8,128)(2,1)S(1)}, bf16[2,128,128]{2,1,0:T(8,128)(2,1)S(1)}, u32[]{:S(2)}, u32[]{:S(2)}) collective-permute-start(bf16[2,128,128]{2,1,0:T(8,128)(2,1)S(1)} %pad_maximum_fusion.7), channel_id=1, source_target_pairs={{0,48},{2,50},{4,52},{6,54},{8,56},{10,58},{12,60},{14,62},{16,32}... | collective-permute-start | bytes 196616 | tf_op jit(solution)/shard_map/ppermute | solution.py:334
  5.6 5.8 %collective-permute-start.2 = (bf16[2,128,128]{2,1,0:T(8,128)(2,1)S(1)}, bf16[2,128,128]{2,1,0:T(8,128)(2,1)S(1)}, u32[]{:S(2)}, u32[]{:S(2)}) collective-permute-start(bf16[2,128,128]{2,1,0:T(8,128)(2,1)S(1)} %pad_maximum_fusion.7), channel_id=1, source_target_pairs={{0,32},{2,34},{4,36},{6,38},{8,40},{10,42},{12,44},{14,46},{16,48}... | collective-permute-start | bytes 196616 | tf_op jit(solution)/shard_map/ppermute | solution.py:334
  6.8 11.7 %collective-permute-start = (bf16[1024,128]{1,0:T(8,128)(2,1)S(1)}, bf16[1024,128]{1,0:T(8,128)(2,1)S(1)}, u32[]{:S(2)}, u32[]{:S(2)}) collective-permute-start(bf16[1024,128]{1,0:T(8,128)(2,1)S(1)} %get-tuple-element.82), channel_id=1, source_target_pairs={{0,48},{2,50},{4,52},{6,54},{8,56},{10,58},{12,60},{14,62},{16,32}... | collective-permute-start | bytes 786440 | tf_op jit(solution)/shard_map/ppermute | solution.py:337
  11.4 12.0 %collective-permute-start.9 = (bf16[4,2,128,128]{3,2,1,0:T(8,128)(2,1)S(1)}, bf16[4,2,128,128]{3,2,1,0:T(8,128)(2,1)S(1)}, u32[]{:S(2)}, u32[]{:S(2)}) collective-permute-start(bf16[4,2,128,128]{3,2,1,0:T(8,128)(2,1)S(1)} %pad_maximum_fusion.2.refs_4_.refs_8_), channel_id=1, source_target_pairs={{0,2},{2,0},{4,6},{6,4},{8,10},{10,8},{12,14},{14,12},{16,18},{18,... | collective-permute-start | bytes 786440 | tf_op jit(solution)/shard_map/ppermute | solution.py:311
  13.4 13.4 %collective-permute-start.5 = (bf16[4,2,128,128]{3,2,1,0:T(8,128)(2,1)S(1)}, bf16[4,2,128,128]{3,2,1,0:T(8,128)(2,1)S(1)}, u32[]{:S(2)}, u32[]{:S(2)}) collective-permute-start(bf16[4,2,128,128]{3,2,1,0:T(8,128)(2,1)S(1)} %pad_maximum_fusion.2.refs_4_.refs_8_), channel_id=1, source_target_pairs={{0,14},{2,4},{4,2},{6,8},{8,6},{10,12},{12,10},{14,0},{16,30},{18,... | collective-permute-start | bytes 786440 | tf_op jit(solution)/shard_map/ppermute | solution.py:315
  21.9 26.3 %collective-permute-start.4 = (bf16[1024,128]{1,0:T(8,128)(2,1)S(1)}, bf16[1024,128]{1,0:T(8,128)(2,1)S(1)}, u32[]{:S(2)}, u32[]{:S(2)}) collective-permute-start(bf16[1024,128]{1,0:T(8,128)(2,1)S(1)} %get-tuple-element.36), channel_id=1, source_target_pairs={{0,48},{2,50},{4,52},{6,54},{8,56},{10,58},{12,60},{14,62},{16,32}... | collective-permute-start | bytes 786440 | tf_op jit(solution)/shard_map/ppermute | solution.py:355
  23.4 7.8 %collective-permute-start.10 = (bf16[4,2,128,128]{3,2,1,0:T(8,128)(2,1)S(1)}, bf16[4,2,128,128]{3,2,1,0:T(8,128)(2,1)S(1)}, u32[]{:S(2)}, u32[]{:S(2)}) collective-permute-start(bf16[4,2,128,128]{3,2,1,0:T(8,128)(2,1)S(1)} %collective-permute-done.9.refs_4_.refs_8_), channel_id=1, source_target_pairs={{0,14},{2,4},{4,2},{6,8},{8,6},{10,12},{12,10},{14,0},{16,30},{18,... | collective-permute-start | bytes 786440 | tf_op jit(solution)/shard_map/ppermute | solution.py:315
  26.9 8.6 %collective-permute-start.6 = (bf16[4,2,128,128]{3,2,1,0:T(8,128)(2,1)S(1)}, bf16[4,2,128,128]{3,2,1,0:T(8,128)(2,1)S(1)}, u32[]{:S(2)}, u32[]{:S(2)}) collective-permute-start(bf16[4,2,128,128]{3,2,1,0:T(8,128)(2,1)S(1)} %collective-permute-done.5.refs_5_.refs_9_), channel_id=1, source_target_pairs={{0,2},{2,0},{4,6},{6,4},{8,10},{10,8},{12,14},{14,12},{16,18},{18,... | collective-permute-start | bytes 786440 | tf_op jit(solution)/shard_map/ppermute | solution.py:311
  31.2 7.7 %collective-permute-start.11 = (bf16[4,2,128,128]{3,2,1,0:T(8,128)(2,1)S(1)}, bf16[4,2,128,128]{3,2,1,0:T(8,128)(2,1)S(1)}, u32[]{:S(2)}, u32[]{:S(2)}) collective-permute-start(bf16[4,2,128,128]{3,2,1,0:T(8,128)(2,1)S(1)} %collective-permute-done.10.refs_5_.refs_9_), channel_id=1, source_target_pairs={{0,2},{2,0},{4,6},{6,4},{8,10},{10,8},{12,14},{14,12},{16,18},{18,... | collective-permute-start | bytes 786440 | tf_op jit(solution)/shard_map/ppermute | solution.py:311
  35.5 9.0 %collective-permute-start.7 = (bf16[4,2,128,128]{3,2,1,0:T(8,128)(2,1)S(1)}, bf16[4,2,128,128]{3,2,1,0:T(8,128)(2,1)S(1)}, u32[]{:S(2)}, u32[]{:S(2)}) collective-permute-start(bf16[4,2,128,128]{3,2,1,0:T(8,128)(2,1)S(1)} %collective-permute-done.6.refs_4_.refs_8_), channel_id=1, source_target_pairs={{0,14},{2,4},{4,2},{6,8},{8,6},{10,12},{12,10},{14,0},{16,30},{18,... | collective-permute-start | bytes 786440 | tf_op jit(solution)/shard_map/ppermute | solution.py:315
  39.0 9.3 %collective-permute-start.12 = (bf16[2,2,128,128]{3,2,1,0:T(8,128)(2,1)S(1)}, bf16[2,2,128,128]{3,2,1,0:T(8,128)(2,1)S(1)}, u32[]{:S(2)}, u32[]{:S(2)}) collective-permute-start(bf16[2,2,128,128]{3,2,1,0:T(8,128)(2,1)S(1)} %slice.92), channel_id=1, source_target_pairs={{0,14},{2,4},{4,2},{6,8},{8,6},{10,12},{12,10},{14,0},{16,30},{18,... | collective-permute-start | bytes 393224 | tf_op jit(solution)/shard_map/ppermute | solution.py:315
  44.5 5.2 %collective-permute-start.8 = (bf16[2,2,128,128]{3,2,1,0:T(8,128)(2,1)S(1)}, bf16[2,2,128,128]{3,2,1,0:T(8,128)(2,1)S(1)}, u32[]{:S(2)}, u32[]{:S(2)}) collective-permute-start(bf16[2,2,128,128]{3,2,1,0:T(8,128)(2,1)S(1)} %slice.91), channel_id=1, source_target_pairs={{0,2},{2,0},{4,6},{6,4},{8,10},{10,8},{12,14},{14,12},{16,18},{18,... | collective-permute-start | bytes 393224 | tf_op jit(solution)/shard_map/ppermute | solution.py:311
  54.6 6.4 %collective-permute-start.14 = (bf16[2,2,128,128]{3,2,1,0:T(8,128)(2,1)S(1)}, bf16[2,2,128,128]{3,2,1,0:T(8,128)(2,1)S(1)}, u32[]{:S(2)}, u32[]{:S(2)}) collective-permute-start(bf16[2,2,128,128]{3,2,1,0:T(8,128)(2,1)S(1)} %get-tuple-element.51), channel_id=1, source_target_pairs={{0,2},{2,0},{4,6},{6,4},{8,10},{10,8},{12,14},{14,12},{16,18},{18,... | collective-permute-start | bytes 393224 | tf_op jit(solution)/shard_map/ppermute | solution.py:311
  54.7 7.4 %collective-permute-start.15 = (bf16[2,2,128,128]{3,2,1,0:T(8,128)(2,1)S(1)}, bf16[2,2,128,128]{3,2,1,0:T(8,128)(2,1)S(1)}, u32[]{:S(2)}, u32[]{:S(2)}) collective-permute-start(bf16[2,2,128,128]{3,2,1,0:T(8,128)(2,1)S(1)} %get-tuple-element.52), channel_id=1, source_target_pairs={{0,14},{2,4},{4,2},{6,8},{8,6},{10,12},{12,10},{14,0},{16,30},{18,... | collective-permute-start | bytes 393224 | tf_op jit(solution)/shard_map/ppermute | solution.py:315
  54.8 11.9 %collective-permute-start.13 = (bf16[1024,128]{1,0:T(8,128)(2,1)S(1)}, bf16[1024,128]{1,0:T(8,128)(2,1)S(1)}, u32[]{:S(2)}, u32[]{:S(2)}) collective-permute-start(bf16[1024,128]{1,0:T(8,128)(2,1)S(1)} %get-tuple-element.50), channel_id=1, source_target_pairs={{0,48},{2,50},{4,52},{6,54},{8,56},{10,58},{12,60},{14,62},{16,32}... | collective-permute-start | bytes 786440 | tf_op jit(solution)/shard_map/ppermute | solution.py:362
  61.1 10.4 %collective-permute-start.16 = (bf16[4,2,128,128]{3,2,1,0:T(8,128)(2,1)S(1)}, bf16[4,2,128,128]{3,2,1,0:T(8,128)(2,1)S(1)}, u32[]{:S(2)}, u32[]{:S(2)}) collective-permute-start(bf16[4,2,128,128]{3,2,1,0:T(8,128)(2,1)S(1)} %pad_maximum_fusion.3), channel_id=1, source_target_pairs={{0,14},{2,4},{4,2},{6,8},{8,6},{10,12},{12,10},{14,0},{16,30},{18,... | collective-permute-start | bytes 786440 | tf_op jit(solution)/shard_map/ppermute | solution.py:315
  62.2 9.6 %collective-permute-start.18 = (bf16[4,2,128,128]{3,2,1,0:T(8,128)(2,1)S(1)}, bf16[4,2,128,128]{3,2,1,0:T(8,128)(2,1)S(1)}, u32[]{:S(2)}, u32[]{:S(2)}) collective-permute-start(bf16[4,2,128,128]{3,2,1,0:T(8,128)(2,1)S(1)} %pad_maximum_fusion.4), channel_id=1, source_target_pairs={{0,2},{2,0},{4,6},{6,4},{8,10},{10,8},{12,14},{14,12},{16,18},{18,... | collective-permute-start | bytes 786440 | tf_op jit(solution)/shard_map/ppermute | solution.py:311
  71.6 8.4 %collective-permute-start.17 = (bf16[4,2,128,128]{3,2,1,0:T(8,128)(2,1)S(1)}, bf16[4,2,128,128]{3,2,1,0:T(8,128)(2,1)S(1)}, u32[]{:S(2)}, u32[]{:S(2)}) collective-permute-start(bf16[4,2,128,128]{3,2,1,0:T(8,128)(2,1)S(1)} %add_convert_fusion.3), channel_id=1, source_target_pairs={{0,2},{2,0},{4,6},{6,4},{8,10},{10,8},{12,14},{14,12},{16,18},{18,... | collective-permute-start | bytes 786440 | tf_op jit(solution)/shard_map/ppermute | solution.py:311
  71.8 8.7 %collective-permute-start.19 = (bf16[4,2,128,128]{3,2,1,0:T(8,128)(2,1)S(1)}, bf16[4,2,128,128]{3,2,1,0:T(8,128)(2,1)S(1)}, u32[]{:S(2)}, u32[]{:S(2)}) collective-permute-start(bf16[4,2,128,128]{3,2,1,0:T(8,128)(2,1)S(1)} %add_convert_fusion.2), channel_id=1, source_target_pairs={{0,14},{2,4},{4,2},{6,8},{8,6},{10,12},{12,10},{14,0},{16,30},{18,... | collective-permute-start | bytes 786440 | tf_op jit(solution)/shard_map/ppermute | solution.py:315
  80.1 7.7 %collective-permute-start.22 = (bf16[4,2,128,128]{3,2,1,0:T(8,128)(2,1)S(1)}, bf16[4,2,128,128]{3,2,1,0:T(8,128)(2,1)S(1)}, u32[]{:S(2)}, u32[]{:S(2)}) collective-permute-start(bf16[4,2,128,128]{3,2,1,0:T(8,128)(2,1)S(1)} %add_convert_fusion), channel_id=1, source_target_pairs={{0,14},{2,4},{4,2},{6,8},{8,6},{10,12},{12,10},{14,0},{16,30},{18,... | collective-permute-start | bytes 786440 | tf_op jit(solution)/shard_map/ppermute | solution.py:315
  80.6 7.2 %collective-permute-start.21 = (bf16[4,2,128,128]{3,2,1,0:T(8,128)(2,1)S(1)}, bf16[4,2,128,128]{3,2,1,0:T(8,128)(2,1)S(1)}, u32[]{:S(2)}, u32[]{:S(2)}) collective-permute-start(bf16[4,2,128,128]{3,2,1,0:T(8,128)(2,1)S(1)} %add_convert_fusion.1), channel_id=1, source_target_pairs={{0,2},{2,0},{4,6},{6,4},{8,10},{10,8},{12,14},{14,12},{16,18},{18,... | collective-permute-start | bytes 786440 | tf_op jit(solution)/shard_map/ppermute | solution.py:311
  84.5 7.7 %collective-permute-start.20 = (bf16[1024,128]{1,0:T(8,128)(2,1)S(1)}, bf16[1024,128]{1,0:T(8,128)(2,1)S(1)}, u32[]{:S(2)}, u32[]{:S(2)}) collective-permute-start(bf16[1024,128]{1,0:T(8,128)(2,1)S(1)} %get-tuple-element.64), channel_id=1, source_target_pairs={{0,48},{2,50},{4,52},{6,54},{8,56},{10,58},{12,60},{14,62},{16,32}... | collective-permute-start | bytes 786440 | tf_op jit(solution)/shard_map/ppermute | solution.py:377
  88.0 5.6 %collective-permute-start.25 = (bf16[2,128,128]{2,1,0:T(8,128)(2,1)S(1)}, bf16[2,128,128]{2,1,0:T(8,128)(2,1)S(1)}, u32[]{:S(2)}, u32[]{:S(2)}) collective-permute-start(bf16[2,128,128]{2,1,0:T(8,128)(2,1)S(1)} %get-tuple-element.85), channel_id=1, source_target_pairs={{0,48},{2,50},{4,52},{6,54},{8,56},{10,58},{12,60},{14,62},{16,32}... | collective-permute-start | bytes 196616 | tf_op jit(solution)/shard_map/ppermute | solution.py:386
  89.9 5.8 %collective-permute-start.24 = (bf16[2,128,128]{2,1,0:T(8,128)(2,1)S(1)}, bf16[2,128,128]{2,1,0:T(8,128)(2,1)S(1)}, u32[]{:S(2)}, u32[]{:S(2)}) collective-permute-start(bf16[2,128,128]{2,1,0:T(8,128)(2,1)S(1)} %get-tuple-element.86), channel_id=1, source_target_pairs={{0,32},{2,34},{4,36},{6,38},{8,40},{10,42},{12,44},{14,46},{16,48}... | collective-permute-start | bytes 196616 | tf_op jit(solution)/shard_map/ppermute | solution.py:386
  (7 other events, 20.0 us)
